TPU v7x, 512 devices: a whole 4x8x8 slice. The times are simulated.
512 devices in a mesh: ens: 16 (over x_lo, y), space: 32 (over x_hi, z, core).
Axes of the slice: x: 4 (x_hi: 2, x_lo: 2; x = x_hi * 2 + x_lo), y: 8, z: 8, core: 2. Of those that a mesh axis runs over, the one named last changes fastest.
Arguments:
- member_embedding: bfloat16 [16, 512, 32, 720], P('ens', None, 'space'), may hold values from -6 to 6
- weights: bfloat16 [9, 100, 512], replicated, may hold values from -0.09375 to 0.09375
- verifying_observed_grid: float32 [100, 32, 720], P(None, 'space', 'ens'), may hold values from -6 to 6
- area_weight: float32 [32], P('space'), may hold values from 0.3 to 3
Outputs:
- crps_objective: float32 [], replicated
- latent_derivative: bfloat16 [16, 512, 32, 720], P('ens', None, 'space')
- grad_weight: float32 [9, 100, 512], replicated
All inputs are finite; a program needn't handle non-finite values.
Results may differ from a plain program's by a relative error of at most 0.0085.
Values may be sent and summed in bfloat16 or wider, within the bound.
A program may use at most 64 MiB of HBM per device.

v0:
```python
import math

import jax
import jax.numpy as jnp
from jax import lax
from jax.sharding import PartitionSpec as P

smoothing = 0.01
fairness = 0.95


def extended(value, sides, width):
    for axis, dim in sides:
        devices, length = (lax.axis_size(axis), value.shape[dim])
        up = [(i, (i + 1) % devices) for i in range(devices - 1)]
        down = [(j, i) for i, j in up]
        last = lax.slice_in_dim(value, length - width, length, axis=dim)
        first = lax.slice_in_dim(value, 0, width, axis=dim)
        before = lax.ppermute(last, axis, up)
        after = lax.ppermute(first, axis, down)
        value = jnp.concatenate([before, value, after], axis=dim)
    return value


def tap_scale(row_values, grid_rows):
    latitude = math.pi * ((row_values.astype(jnp.float32) + 0.5) / grid_rows - 0.5)
    east_west = 1.0 / (0.25 + jnp.cos(latitude))
    plain = jnp.ones_like(east_west)
    scales = []
    for tap_index in range(9):
        row_off = tap_index // 3 - 1
        col_off = tap_index % 3 - 1
        scales.append(east_west if row_off == 0 and col_off != 0 else plain)
    return jnp.stack(scales)


def per_device(member_embedding, weights, verifying_observed_grid, area_weight):
    field = member_embedding[0]
    internal_embedding, band_rows, longitudes = field.shape
    feature_sequence = weights.shape[1]
    members = lax.axis_size("ens")
    grid_rows = band_rows * lax.axis_size("space")
    rows_index = lax.axis_index("space") * band_rows + jnp.arange(band_rows, dtype=jnp.int32)
    scales = tap_scale(rows_index, grid_rows)
    padded = extended(field, (("space", 1),), 1)
    overall_accumulated = jnp.zeros((feature_sequence, band_rows, longitudes), jnp.float32)
    for tap_index in range(9):
        row_off = tap_index // 3 - 1
        col_off = tap_index % 3 - 1
        source = jnp.roll(padded[:, 1 + row_off : 1 + row_off + band_rows, :], -col_off, axis=2)
        product = jnp.dot(
            weights[tap_index],
            source.reshape(internal_embedding, -1),
            preferred_element_type=jnp.float32,
        )
        overall_accumulated = (
            overall_accumulated
            + product.reshape(feature_sequence, band_rows, longitudes)
            * scales[tap_index][None, :, None]
        )
    outcome_grids = overall_accumulated.astype(jnp.bfloat16)
    collected_rows = lax.all_to_all(
        outcome_grids[None], "ens", split_axis=3, concat_axis=0, tiled=True
    )
    values = collected_rows.astype(jnp.float32)
    epsilon = (1.0 - fairness) / members
    pair_coef = (1.0 - epsilon) / (members - 1)
    diff_obs = values - verifying_observed_grid[None]
    root_obs = jnp.sqrt(diff_obs * diff_obs + smoothing)

    def add_member(member, totals):
        pair_grad, pair_sum = totals
        other = lax.dynamic_index_in_dim(values, member, 0, keepdims=False)
        delta = values - other[None]
        root = jnp.sqrt(delta * delta + smoothing)
        return (pair_grad + delta / root, pair_sum + jnp.sum(root, axis=0))

    empty_zeros = jnp.zeros_like(values)
    pair_grad, pair_sum = lax.fori_loop(0, members, add_member, (empty_zeros, empty_zeros[0]))
    crps = jnp.sum(root_obs, axis=0) - 0.5 * pair_coef * pair_sum
    loss_part = jnp.sum(area_weight[None, :, None] * crps)
    gradient = (
        area_weight[None, None, :, None] * (diff_obs / root_obs - pair_coef * pair_grad)
    ).astype(jnp.bfloat16)
    grad_field = lax.all_to_all(gradient, "ens", split_axis=0, concat_axis=3, tiled=True)[0]
    updates = []
    for tap_index in range(9):
        row_off = tap_index // 3 - 1
        col_off = tap_index % 3 - 1
        source = jnp.roll(padded[:, 1 + row_off : 1 + row_off + band_rows, :], -col_off, axis=2)
        outer = jnp.einsum("crl,krl->rck", grad_field, source, preferred_element_type=jnp.float32)
        updates.append(jnp.sum(outer * scales[tap_index][:, None, None], axis=0))
    weight_part = jnp.stack(updates)
    grad_pad = extended(grad_field, (("space", 1),), 1)
    grad_total = jnp.zeros((internal_embedding, band_rows, longitudes), jnp.float32)
    for tap_index in range(9):
        row_off = tap_index // 3 - 1
        col_off = tap_index % 3 - 1
        earlier = jnp.roll(grad_pad[:, 1 - row_off : 1 - row_off + band_rows, :], col_off, axis=2)
        moved = jnp.dot(
            weights[tap_index].T,
            earlier.reshape(feature_sequence, -1),
            preferred_element_type=jnp.float32,
        )
        shifted_scale = tap_scale(rows_index - row_off, grid_rows)[tap_index]
        grad_total = (
            grad_total
            + moved.reshape(internal_embedding, band_rows, longitudes)
            * shifted_scale[None, :, None]
        )
    aggregate_coefficient, loss_sum = lax.psum((weight_part, loss_part), ("ens", "space"))
    tally_number = members * grid_rows * longitudes
    return (
        loss_sum / tally_number,
        grad_total.astype(jnp.bfloat16)[None],
        aggregate_coefficient / tally_number,
    )


def solution(mesh):
    return jax.shard_map(
        per_device,
        mesh=mesh,
        in_specs=(P("ens", None, "space", None), P(), P(None, "space", "ens"), P("space")),
        out_specs=(P(), P("ens", None, "space", None), P()),
        check_vma=False,
    )
```

profile of v0, /device:TPU:1, one launch (start us, length us, event | category | flops | bytes accessed | tf_op | source)
XLA Modules:
  0.0 479.0 jit_solution(492689472682160652)
XLA Ops:
  7.2 8.9 %collective-permute-start.1 = (bf16[512,1,720]{0,2,1:T(8,128)(2,1)}, bf16[512,1,720]{0,2,1:T(8,128)(2,1)S(1)}, u32[]{:S(2)}, u32[]{:S(2)}) collective-permute-start(bf16[512,1,720]{0,2,1:T(8,128)(2,1)} %bitcast.246), channel_id=1, source_target_pairs={{1,0},{2,1},{3,2},{4,3},{5,4},{6,5},{7,6},{8,7},{9,8},{10,9},{11,1... | collective-permute-start | bytes 2211848 | tf_op jit(solution)/shard_map/ppermute | solution.py:20
  16.1 1.9 collective-permute-start
  18.0 2.4 fusion.116
  20.6 1.6 fusion.2
  22.7 4.1 collective-permute-done
  31.9 1.8 reduce.4
  34.5 4.5 all-to-all-start
  39.7 6.8 %all-to-all-done = bf16[16,2,2250]{2,1,0:T(2,128)(2,1)S(1)} async-done(((bf16[16,2,2250]{2,1,0:T(2,128)(2,1)}), bf16[16,2,2250]{2,1,0:T(2,128)(2,1)S(1)}, u32[]{:S(2)}, u32[]{:S(2)}) %all-to-all-start) | async-done | bytes 144032 | tf_op jit(solution)/shard_map/all_to_all | solution.py:62
  47.2 5.0 %while.16 = (s32[]{:T(128)}, f32[16,100,1,45]{1,3,2,0:T(8,128)S(1)}, f32[100,1,45]{0,2,1:T(8,128)S(1)}, f32[16,100,1,45]{1,3,2,0:T(8,128)S(1)}, s32[]{:T(128)}, /*index=5*/s32[]{:T(128)}) while((s32[]{:T(128)}, f32[16,100,1,45]{1,3,2,0:T(8,128)S(1)}, f32[100,1,45]{0,2,1:T(8,128)S(1)}, f32[16,100,1,45]{1,3,2,0:T(8,128)S(1)}, ...), condition=%wide.region_3.4_spmd.clone, body=%wide.region_1.3_spmd.clone.sunk | while | flops 508503 | bytes 990092 | solution.py:79
  52.1 1.9 multiply_convert_fusion
  54.1 1.8 reduce.5
  56.9 3.5 all-to-all-start.1
  61.0 110.5 %psum.14 = f32[]{:T(128)} all-reduce(f32[]{:T(128)} %fusion.94), channel_id=1, replica_groups=mesh['ens'=16,'space'=32] {'ens','space'}, use_global_device_ids=true, to_apply=%region_5.6 | all-reduce | flops 1 | bytes 8 | tf_op jit(solution)/shard_map/psum | solution.py:111
  174.2 2.6 collective-permute-start.3
  176.8 2.1 collective-permute-start.2
  178.9 1.8 fusion.123
  180.7 1.0 fusion.21
  181.7 2.4 fusion.64
  186.1 1.0 fusion.18
  189.1 1.0 fusion.13
  191.1 1.0 fusion.11
  196.0 1.6 fusion.32
  197.5 270.5 %all-reduce.2.cloned.1.call-done = f32[9,100,512]{2,1,0:T(8,128)} async-done(((f32[9,100,512]{2,1,0:T(8,128)}), f32[9,100,512]{2,1,0:T(8,128)}) %all-reduce.2.cloned.1.call-update) | async-done | bytes 1843216 | tf_op jit(solution)/shard_map/psum | solution.py:111
  468.0 3.0 broadcast_multiply_fusion
  (136 shorter events, 23.5 us)
Async XLA Ops:
  7.2 13.4 %copy-start = (bf16[1,512,1,720]{1,3,2,0:T(8,128)(2,1)S(1)}, bf16[1,512,1,720]{1,3,2,0:T(8,128)(2,1)}, u32[]{:S(2)}) copy-start(bf16[1,512,1,720]{1,3,2,0:T(8,128)(2,1)} %param.6) | copy-start | bytes 2211844
  7.2 20.2 %collective-permute-start.1 = (bf16[512,1,720]{0,2,1:T(8,128)(2,1)}, bf16[512,1,720]{0,2,1:T(8,128)(2,1)S(1)}, u32[]{:S(2)}, u32[]{:S(2)}) collective-permute-start(bf16[512,1,720]{0,2,1:T(8,128)(2,1)} %bitcast.246), channel_id=1, source_target_pairs={{1,0},{2,1},{3,2},{4,3},{5,4},{6,5},{7,6},{8,7},{9,8},{10,9},{11,1... | collective-permute-start | bytes 2211848 | tf_op jit(solution)/shard_map/ppermute | solution.py:20
  16.1 10.6 %collective-permute-start = (bf16[512,1,720]{0,2,1:T(8,128)(2,1)}, bf16[512,1,720]{0,2,1:T(8,128)(2,1)S(1)}, u32[]{:S(2)}, u32[]{:S(2)}) collective-permute-start(bf16[512,1,720]{0,2,1:T(8,128)(2,1)} %bitcast.247), channel_id=1, source_target_pairs={{0,1},{1,2},{2,3},{3,4},{4,5},{5,6},{6,7},{7,8},{8,9},{9,10},{10,1... | collective-permute-start | bytes 2211848 | tf_op jit(solution)/shard_map/ppermute | solution.py:19
  20.5 8.7 %copy-start.6 = (bf16[512,1,719]{0,2,1:T(8,128)(2,1)}, bf16[512,1,719]{0,2,1:T(8,128)(2,1)S(1)}, u32[]{:S(2)}) copy-start(bf16[512,1,719]{0,2,1:T(8,128)(2,1)S(1)} %get-tuple-element.124) | copy-start | bytes 2208772
  20.6 1.7 copy-start.8
  26.9 1.8 copy-start.4
  28.0 1.2 copy-start.11
  28.0 1.9 copy-start.2
  30.0 9.7 %copy-start.17 = (f32[100,1,45]{0,1,2:T(1,128)S(1)}, f32[100,1,45]{0,1,2:T(1,128)}, u32[]{:S(2)}) copy-start(f32[100,1,45]{0,1,2:T(1,128)} %param.8) | copy-start | bytes 54004
  34.5 11.9 %all-to-all-start = ((bf16[16,2,2250]{2,1,0:T(2,128)(2,1)}), bf16[16,2,2250]{2,1,0:T(2,128)(2,1)S(1)}, u32[]{:S(2)}, u32[]{:S(2)}) async-start(bf16[16,2,2250]{2,1,0:T(2,128)(2,1)} %reshape.297), calls=%async_computation | async-start | bytes 294912 | tf_op jit(solution)/shard_map/all_to_all | solution.py:62
  56.9 115.3 %all-to-all-start.1 = ((bf16[16,2,2250]{2,1,0:T(2,128)(2,1)}), bf16[16,2,2250]{2,1,0:T(2,128)(2,1)S(1)}, u32[]{:S(2)}, u32[]{:S(2)}) async-start(bf16[16,2,2250]{2,1,0:T(2,128)(2,1)} %reshape.299), calls=%async_computation.1 | async-start | bytes 294912 | tf_op jit(solution)/shard_map/all_to_all | solution.py:85
  60.4 407.6 %all-reduce.2.cloned.1.call-start = ((), (), s32[]{:S(2)}) async-start(), calls=%async_computation.2 | async-start | bytes 3833856 | tf_op jit(solution)/shard_map/psum | solution.py:111
  172.2 8.5 %copy-start.5 = (bf16[512,1,719]{0,2,1:T(8,128)(2,1)S(1)}, bf16[512,1,719]{0,2,1:T(8,128)(2,1)}, u32[]{:S(2)}) copy-start(bf16[512,1,719]{0,2,1:T(8,128)(2,1)} %copy-done.4) | copy-start | bytes 2208772
  174.2 19.7 %collective-permute-start.3 = (bf16[100,1,720]{0,2,1:T(8,128)(2,1)}, bf16[100,1,720]{0,2,1:T(8,128)(2,1)S(1)}, u32[]{:S(2)}, u32[]{:S(2)}) collective-permute-start(bf16[100,1,720]{0,2,1:T(8,128)(2,1)} %squeeze.58), channel_id=1, source_target_pairs={{0,1},{1,2},{2,3},{3,4},{4,5},{5,6},{6,7},{7,8},{8,9},{9,10},{10,1... | collective-permute-start | bytes 432008 | tf_op jit(solution)/shard_map/ppermute | solution.py:19
  176.8 16.6 %collective-permute-start.2 = (bf16[100,1,720]{0,2,1:T(8,128)(2,1)}, bf16[100,1,720]{0,2,1:T(8,128)(2,1)S(1)}, u32[]{:S(2)}, u32[]{:S(2)}) collective-permute-start(bf16[100,1,720]{0,2,1:T(8,128)(2,1)} %squeeze.58), channel_id=1, source_target_pairs={{1,0},{2,1},{3,2},{4,3},{5,4},{6,5},{7,6},{8,7},{9,8},{10,9},{11,1... | collective-permute-start | bytes 432008 | tf_op jit(solution)/shard_map/ppermute | solution.py:20
  181.7 3.4 copy-start.14
  184.1 1.9 copy-start.7
  186.1 2.0 copy-start.10
  187.1 1.9 copy-start.3
  189.1 2.0 copy-start.12
  191.1 1.2 copy-start.9
  191.1 1.3 copy-start.16
  192.1 1.0 copy-start.15
  194.6 1.4 copy-start.1
  (1 other events, 0.9 us)
Sparse Core Ops, SparseCore 0:
  192.2 275.7 all-reduce.1
where the time goes:
time: 481 us; the launch traced here: 479 us
  waiting for transfers between devices  281 us (58%)
  blocking collectives  111 us (23%)
  starting transfers between devices  23.6 us (5%)
  matrix products  19.8 us (4%)
  between operations  17 us (4%)
  other arithmetic  13.7 us (3%)
  local copies, waits for them, and re-layouts  12.4 us (3%)
    psum x1, waiting for transfers between devices, per_device(): lax.psum((weight_part, loss_part), ('ens', 'space'))  270 us
    psum x1, blocking collectives, per_device(): lax.psum((weight_part, loss_part), ('ens', 'space'))  111 us
    ppermute x2, starting transfers between devices, extended(): after = lax.ppermute(first, axis, down)  11 us
  transfers between devices with their start and end apart: 7, of which 3 were waited for; matrix products, arithmetic and copies ran while one was open for 5% of the time, Pallas kernels for 0%

commit v1 on v0

v1 whole, which is shorter than its diff:
```python
import functools
import math

import jax
import jax.numpy as jnp
from jax import lax
from jax.experimental import pallas as pl
from jax.experimental.pallas import tpu as pltpu
from jax.sharding import PartitionSpec as P

MESH = pl.DeviceIdType.MESH
F32 = jnp.float32
BF16 = jnp.bfloat16

CH, LATENT, LON, MEMBERS, NLAT = 100, 512, 720, 16, 32
LANES = 128
BLOCK = LON // MEMBERS
SLOT = 48
RING = 8
TAP_ROWS = 112
HALF = LATENT // 2
SMOOTHING = 0.01
PAIR_COEF = (1.0 - 0.05 / MEMBERS) / (MEMBERS - 1)
COLUMNS = (4, 0, 1, 2, 6, 7, 8, 3, 5)


def remote(src, dst, send_sem, recv_sem, device):
    return pltpu.make_async_remote_copy(
        src_ref=src, dst_ref=dst, send_sem=send_sem, recv_sem=recv_sem,
        device_id=device, device_id_type=MESH,
    )


def resplit(block):
    total = block[0:1] + block[1:2]
    lead = total.astype(BF16).astype(F32)
    row = lax.broadcasted_iota(jnp.int32, block.shape, 0)
    return jnp.where(row == 0, lead, jnp.where(row == 1, total - lead, block))


def kernel(area_ref, emb, w_ref, obs, d_ref, red,
           wp, ps, pr, fbuf, send_a, recv_a, vals, send_b, recv_b, gs, gr, gf, gcat,
           dwh, send_c, recv_c, s1, r1, s2, r2, s3, r3,
           h_send, h_recv, a_send, a_recv, b_send, b_recv, g_send, g_recv,
           c_send, c_recv, s1_send, s1_recv, s2_send, s2_recv, s3_send, s3_recv,
           t2_send, t2_recv, t1_send, t1_recv, tc_send, tc_recv):
    me = lax.axis_index("ens")
    row = lax.axis_index("space")
    x_lo, y = me // RING, me % RING
    core = row % 2
    z = (row // 2) % RING
    x_hi = row // (2 * RING)
    x = 2 * x_hi + x_lo
    up = (row + 1) % NLAT
    down = (row + NLAT - 1) % NLAT
    twin = (me, row + 1 - 2 * core)

    def at(x_, y_, z_):
        return ((x_ % 2) * RING + y_, ((x_ // 2) * RING + z_) * 2 + core)

    pos1 = y + core * (z - y)
    pos2 = z + core * (y - z)

    def ring1(p):
        return at(x, y + (1 - core) * (p - y), z + core * (p - z))

    def ring2(p):
        return at(x, y + core * (p - y), z + (1 - core) * (p - z))

    barrier = pltpu.get_barrier_semaphore()

    def greet(device):
        pl.semaphore_signal(barrier, inc=1, device_id=device, device_id_type=MESH)

    @pl.loop(1, MEMBERS)
    def _(i):
        greet(((me + i) % MEMBERS, row))

    @pl.loop(1, RING)
    def _(i):
        greet(at(x, y, (z + i) % RING))

    greet(at((x + 2) % 4, y, z))
    greet(at((x + 2) % 4 + 1 - 2 * (x % 2), y, z))
    greet(twin)
    greet((me, (row + 2 * core - 1 + NLAT) % NLAT))

    wp[...] = jnp.zeros_like(wp)
    for t in range(9):
        wp[t, 0:CH, :] = w_ref[t]

    latitude = math.pi * ((row.astype(F32) + 0.5) / NLAT - 0.5)
    east_west = 1.0 / (0.25 + jnp.cos(jnp.full((1, LANES), latitude, F32)))

    def product(first):
        mat = wp[first:first + 3].reshape(3 * LANES, LATENT)
        out = lax.dot_general(emb[...], mat, (((1,), (1,)), ((), ())), preferred_element_type=F32)
        return (pltpu.roll(out[:, 0:LANES], 1, 0), out[:, LANES:2 * LANES],
                pltpu.roll(out[:, 2 * LANES:3 * LANES], LON - 1, 0))

    west, mid, east = product(6)
    ps[0] = (west + mid + east).astype(BF16)
    pl.semaphore_wait(barrier, MEMBERS - 1 + RING - 1 + 4)
    to_down = remote(ps.at[0], pr.at[0], h_send.at[0], h_recv.at[0], (me, down))
    to_down.start()
    west, mid, east = product(0)
    ps[1] = (west + mid + east).astype(BF16)
    to_up = remote(ps.at[1], pr.at[1], h_send.at[1], h_recv.at[1], (me, up))
    to_up.start()
    west, mid, east = product(3)
    own = mid + east_west * (west + east)
    to_down.wait_recv()
    own = own + jnp.where(row < NLAT - 1, pr[0].astype(F32), 0.0)
    to_up.wait_recv()
    fbuf[0:LON, :] = own + jnp.where(row > 0, pr[1].astype(F32), 0.0)
    fbuf[LON:LON + 16, :] = jnp.zeros((16, LANES), F32)

    for k in range(MEMBERS):
        send_a[k] = fbuf[BLOCK * k:BLOCK * k + SLOT, :].astype(BF16)

    def a_copy(k, slot):
        return remote(send_a.at[k], recv_a.at[slot], a_send.at[k], a_recv.at[slot], (k, row))

    @pl.loop(1, MEMBERS)
    def _(i):
        a_copy((me + i) % MEMBERS, me).start()

    vals[me] = send_a[me].astype(F32)

    @pl.loop(1, MEMBERS)
    def _(i):
        k = (me + i) % MEMBERS
        a_copy(k, k).wait_recv()
        vals[k] = recv_a[k].astype(F32)

    area = area_ref[0]

    def score(j, loss):
        rows = pl.ds(pl.multiple_of(8 * j, 8), 8)
        f = [vals[i, rows, :] for i in range(MEMBERS)]
        o = obs[rows, :]
        grad, pair, total = [], [None] * MEMBERS, None
        pairs = None
        for i in range(MEMBERS):
            d = f[i] - o
            q = d * d + SMOOTHING
            r = lax.rsqrt(q)
            grad.append(d * r)
            total = q * r if total is None else total + q * r
        for i in range(MEMBERS):
            for k in range(i + 1, MEMBERS):
                d = f[i] - f[k]
                q = d * d + SMOOTHING
                r = lax.rsqrt(q)
                u = d * r
                pair[i] = u if pair[i] is None else pair[i] + u
                pair[k] = -u if pair[k] is None else pair[k] - u
                pairs = q * r if pairs is None else pairs + q * r
        for i in range(MEMBERS):
            vals[i, rows, :] = area * (grad[i] - PAIR_COEF * pair[i])
        crps = total - 0.5 * PAIR_COEF * (2.0 * pairs + MEMBERS * math.sqrt(SMOOTHING))
        lon = 8 * j + lax.broadcasted_iota(jnp.int32, (8, LANES), 0)
        ch = lax.broadcasted_iota(jnp.int32, (8, LANES), 1)
        return loss + jnp.where((lon < BLOCK) & (ch < CH), crps, 0.0)

    loss = lax.fori_loop(0, SLOT // 8, score, jnp.zeros((8, LANES), F32))
    loss = area * jnp.sum(loss)

    def b_copy(k, slot):
        return remote(send_b.at[k], recv_b.at[slot], b_send.at[k], b_recv.at[slot], (k, row))

    @pl.loop(1, MEMBERS)
    def _(i):
        k = (me + i) % MEMBERS
        send_b[k] = vals[k].astype(BF16)
        b_copy(k, me).start()

    recv_b[me] = vals[me].astype(BF16)

    sub = lax.broadcasted_iota(jnp.int32, (16, HALF), 0)
    lead = jnp.full((16, HALF), loss, F32).astype(BF16).astype(F32)
    tail = jnp.where(sub == 0, lead, jnp.where(sub == 1, loss - lead, 0.0))
    for h in range(2):
        dwh[h, 9 * TAP_ROWS:, :] = tail
        send_c[h, 9 * TAP_ROWS:, :] = tail.astype(BF16)

    @pl.loop(1, MEMBERS)
    def _(i):
        k = (me + i) % MEMBERS
        b_copy(k, k).wait_recv()

    def wrap(slot):
        gf[slot, 7:8, :] = gf[slot, LON + 7:LON + 8, :]
        gf[slot, LON + 8:LON + 9, :] = gf[slot, 8:9, :]

    for k in range(MEMBERS):
        gf[0, 8 + BLOCK * k:8 + BLOCK * k + SLOT, :] = recv_b[k].astype(F32)
    gs[...] = gf[0, 8:8 + LON, :].astype(BF16)
    g_down = remote(gs, gr.at[0], g_send.at[0], g_recv.at[0], (me, down))
    g_up = remote(gs, gr.at[1], g_send.at[1], g_recv.at[1], (me, up))
    g_down.start()
    g_up.start()
    wrap(0)

    def gather(slot, first):
        for b in range(3):
            column = COLUMNS.index(first + b) * LANES
            gcat[:, column:column + LANES] = gf[slot, 9 - b:9 - b + LON, :].astype(BF16)

    def outer(t):
        column = COLUMNS.index(t) * LANES
        out = lax.dot_general(gcat[:, column:column + LANES], emb[...], (((0,), (0,)), ((), ())),
                              preferred_element_type=F32)[0:TAP_ROWS]
        if t in (3, 5):
            out = out * east_west[:, 0:1]
        for h in range(2):
            part = out[:, HALF * h:HALF * (h + 1)]
            dwh[h, TAP_ROWS * t:TAP_ROWS * (t + 1), :] = part
            send_c[h, TAP_ROWS * t:TAP_ROWS * (t + 1), :] = part.astype(BF16)

    gather(0, 3)
    for t in (3, 4, 5):
        outer(t)
    g_down.wait_recv()
    gf[1, 8:8 + LON, :] = jnp.where(row < NLAT - 1, gr[0].astype(F32), 0.0)
    wrap(1)
    gather(1, 0)
    for t in (0, 1, 2):
        outer(t)
    g_up.wait_recv()
    gf[2, 8:8 + LON, :] = jnp.where(row > 0, gr[1].astype(F32), 0.0)
    wrap(2)
    gather(2, 6)
    for t in (6, 7, 8):
        outer(t)

    rows1 = RING * 16

    def c_copy(p):
        rows = pl.ds(pl.multiple_of(p * rows1, rows1), rows1)
        return remote(send_c.at[1 - core, rows], recv_c.at[rows], c_send.at[p], c_recv.at[p], twin)

    @pl.loop(0, RING)
    def _(i):
        c_copy((pos1 + 1 + i) % RING).start()

    def s1_copy(p, slot):
        return remote(s1.at[p], r1.at[slot], s1_send.at[p], s1_recv.at[slot], ring1(p))

    def chip_sum(p):
        c_copy(p).wait_recv()
        rows = pl.ds(pl.multiple_of(p * rows1, rows1), rows1)
        total = dwh[core, rows, :] + recv_c[rows, :].astype(F32)
        last = total[rows1 - 16:]
        last = jnp.where(p == RING - 1, resplit(last), last)
        return jnp.concatenate([total[:rows1 - 16], last], axis=0).astype(BF16)

    @pl.loop(1, RING)
    def _(i):
        p = (pos1 + i) % RING
        s1[p] = chip_sum(p)
        s1_copy(p, pos1).start()

    r1[pos1] = chip_sum(pos1)

    plain = jnp.concatenate([wp[t] for t in COLUMNS[:7]], axis=0)
    scaled = jnp.concatenate([wp[t] for t in COLUMNS[7:]], axis=0)
    moved = jnp.dot(gcat[:, 0:7 * LANES], plain, preferred_element_type=F32)
    moved_ew = jnp.dot(gcat[:, 7 * LANES:], scaled, preferred_element_type=F32)
    d_ref[...] = (moved + east_west[:, 0:1] * moved_ew).astype(BF16)

    @pl.loop(1, RING)
    def _(i):
        p = (pos1 + i) % RING
        s1_copy(p, p).wait_recv()

    total = r1[0].astype(F32)
    for p in range(1, RING):
        total = total + r1[p].astype(F32)
    last = total[rows1 - 16:]
    last = jnp.where(pos1 == RING - 1, resplit(last), last)
    for q in range(RING - 1):
        s2[q] = total[16 * q:16 * (q + 1)].astype(BF16)
    s2[RING - 1] = last.astype(BF16)

    def s2_copy(p, slot):
        return remote(s2.at[p], r2.at[slot], s2_send.at[p], s2_recv.at[slot], ring2(p))

    @pl.loop(1, RING)
    def _(i):
        s2_copy((pos2 + i) % RING, pos2).start()

    r2[pos2] = s2[pos2]

    @pl.loop(1, RING)
    def _(i):
        p = (pos2 + i) % RING
        s2_copy(p, p).wait_recv()

    special = (pos1 == RING - 1) & (pos2 == RING - 1)
    total = r2[0].astype(F32)
    for p in range(1, RING):
        total = total + r2[p].astype(F32)
    total = jnp.where(special, resplit(total), total).astype(BF16)
    s3[...] = total

    def s3_copy(i, slot):
        p = (x + i) % 4
        return remote(s3, r3.at[slot], s3_send.at[i], s3_recv.at[slot], at(p, y, z))

    @pl.loop(1, 4)
    def _(i):
        s3_copy(i, x).start()

    r3[x] = total

    @pl.loop(1, 4)
    def _(i):
        s3_copy(i, (x + i) % 4).wait_recv()

    total = (r3[0].astype(F32) + r3[1].astype(F32)) + (r3[2].astype(F32) + r3[3].astype(F32))
    total = jnp.where(special, resplit(total), total).astype(BF16)
    red[core, pos1, pos2] = total

    def t2_copy(i, slot):
        block = red.at[core, pos1, slot]
        return remote(block, block, t2_send.at[i], t2_recv.at[slot], ring2((pos2 + i) % RING))

    @pl.loop(1, RING)
    def _(i):
        t2_copy(i, pos2).start()

    @pl.loop(1, RING)
    def _(i):
        t2_copy(i, (pos2 + i) % RING).wait_recv()

    def t1_copy(i, slot):
        block = red.at[core, slot]
        return remote(block, block, t1_send.at[i], t1_recv.at[slot], ring1((pos1 + i) % RING))

    @pl.loop(1, RING)
    def _(i):
        t1_copy(i, pos1).start()

    def tc_copy(half, p):
        block = red.at[half, p]
        return remote(block, block, tc_send.at[p], tc_recv.at[p], twin)

    tc_copy(core, pos1).start()

    @pl.loop(1, RING)
    def _(i):
        p = (pos1 + i) % RING
        t1_copy(i, p).wait_recv()
        tc_copy(core, p).start()

    @pl.loop(0, RING)
    def _(p):
        tc_copy(1 - core, p).wait_recv()

    to_down.wait_send()
    to_up.wait_send()
    g_down.wait_send()
    g_up.wait_send()

    @pl.loop(1, MEMBERS)
    def _(i):
        k = (me + i) % MEMBERS
        a_copy(k, me).wait_send()
        b_copy(k, me).wait_send()

    @pl.loop(0, RING)
    def _(p):
        c_copy(p).wait_send()
        tc_copy(core, p).wait_send()

    @pl.loop(1, RING)
    def _(i):
        s1_copy((pos1 + i) % RING, pos1).wait_send()
        s2_copy((pos2 + i) % RING, pos2).wait_send()
        t2_copy(i, pos2).wait_send()
        t1_copy(i, pos1).wait_send()

    @pl.loop(1, 4)
    def _(i):
        s3_copy(i, x).wait_send()


def per_device(member_embedding, weights, verifying_observed_grid, area_weight):
    emb = member_embedding[0, :, 0, :].T
    obs = jnp.pad(verifying_observed_grid[:, 0, :].T, ((0, SLOT - BLOCK), (0, LANES - CH)))
    vmem = pl.BlockSpec(memory_space=pltpu.VMEM)
    dma = lambda n: pltpu.SemaphoreType.DMA((n,))
    scratch = [
        pltpu.VMEM((9, LANES, LATENT), BF16),
        pltpu.VMEM((2, LON, LANES), BF16),
        pltpu.VMEM((2, LON, LANES), BF16),
        pltpu.VMEM((LON + 16, LANES), F32),
        pltpu.VMEM((MEMBERS, SLOT, LANES), BF16),
        pltpu.VMEM((MEMBERS, SLOT, LANES), BF16),
        pltpu.VMEM((MEMBERS, SLOT, LANES), F32),
        pltpu.VMEM((MEMBERS, SLOT, LANES), BF16),
        pltpu.VMEM((MEMBERS, SLOT, LANES), BF16),
        pltpu.VMEM((LON, LANES), BF16),
        pltpu.VMEM((2, LON, LANES), BF16),
        pltpu.VMEM((3, LON + 32, LANES), F32),
        pltpu.VMEM((LON, 9 * LANES), BF16),
        pltpu.VMEM((2, RING * RING * 16, HALF), F32),
        pltpu.VMEM((2, RING * RING * 16, HALF), BF16),
        pltpu.VMEM((RING * RING * 16, HALF), BF16),
        pltpu.VMEM((RING, RING * 16, HALF), BF16),
        pltpu.VMEM((RING, RING * 16, HALF), BF16),
        pltpu.VMEM((RING, 16, HALF), BF16),
        pltpu.VMEM((RING, 16, HALF), BF16),
        pltpu.VMEM((16, HALF), BF16),
        pltpu.VMEM((4, 16, HALF), BF16),
    ]
    sems = [dma(n) for n in (2, 2, 16, 16, 16, 16, 2, 2, 8, 8, 8, 8, 8, 8, 4, 4, 8, 8, 8, 8, 8, 8)]
    moved, red = pl.pallas_call(
        kernel,
        out_shape=(jax.ShapeDtypeStruct((LON, LATENT), BF16),
                   jax.ShapeDtypeStruct((2, RING, RING, 16, HALF), BF16)),
        in_specs=[pl.BlockSpec(memory_space=pltpu.SMEM), vmem, vmem, vmem],
        out_specs=(vmem, vmem),
        scratch_shapes=scratch + sems,
        compiler_params=pltpu.CompilerParams(
            collective_id=0, has_side_effects=True, vmem_limit_bytes=48 * 1024 * 1024),
        cost_estimate=pl.CostEstimate(flops=2_600_000_000, bytes_accessed=6_000_000, transcendentals=1_000_000),
        name="decoder",
    )(area_weight, emb, weights, obs)
    red = red.reshape(2, RING * RING * 16, HALF)
    tally = MEMBERS * NLAT * LON
    tail = red[0, 9 * TAP_ROWS:9 * TAP_ROWS + 2, 0].astype(F32)
    objective = (tail[0] + tail[1]) / tally
    both = red[:, :9 * TAP_ROWS].reshape(2, 9, TAP_ROWS, HALF)[:, :, :CH].astype(F32) / tally
    grad_weight = jnp.concatenate([both[0], both[1]], axis=-1)
    return objective, moved.T[None, :, None, :], grad_weight


def solution(mesh):
    return jax.shard_map(
        per_device,
        mesh=mesh,
        in_specs=(P("ens", None, "space", None), P(), P(None, "space", "ens"), P("space")),
        out_specs=(P(), P("ens", None, "space", None), P()),
        check_vma=False,
    )
```

time: 481 us -> 91.9 us (0.19)
  waiting for transfers between devices: 281 us -> 0 us
  blocking collectives: 111 us -> 0 us
  Pallas kernels: 0 us -> 81.5 us
  starting transfers between devices: 23.6 us -> 0 us
  matrix products: 19.8 us -> 0 us
  between operations: 17 us -> 3.75 us
  other arithmetic: 13.7 us -> 1.72 us
  local copies, waits for them, and re-layouts: 12.4 us -> 4.63 us
    psum x1 -> x0, waiting for transfers between devices: 270 us -> none  [per_device(): lax.psum((weight_part, loss_part), ('ens', 'space'))]
    psum x1 -> x0, blocking collectives: 111 us -> none  [per_device(): lax.psum((weight_part, loss_part), ('ens', 'space'))]
    pallas_call x0 -> x1, Pallas kernels: none -> 81.5 us  [per_device(): pl.pallas_call(kernel, out_shape=(jax.ShapeDtypeStruct((LON, LATENT), BF1...]
    dot_general x27 -> x0, matrix products: 19.8 us -> none  [the longest x9 8.96 us: per_device(): jnp.einsum('crl,krl->rck', grad_field, source, preferred_element_type=jnp...]
    ppermute x4 -> x0, starting transfers between devices: 15.6 us -> none  [the longest x2 11 us: extended(): after = lax.ppermute(first, axis, down)]
    all_to_all x2 -> x0, starting transfers between devices: 7.97 us -> none  [the longest x1 4.45 us: per_device(): lax.all_to_all(outcome_grids[None], 'ens', split_axis=3, concat_axis=0, t...]
    all_to_all x2 -> x0, waiting for transfers between devices: 6.75 us -> none  [the longest x1 6.75 us: per_device(): lax.all_to_all(outcome_grids[None], 'ens', split_axis=3, concat_axis=0, t...]
    slice x12 -> x2, local copies, waits for them, and re-layouts: 5.46 us -> 0.59 us  [the longest x1 0.52 us: per_device(): objective = (tail[0] + tail[1]) / tally]
  transfers between devices with their start and end apart: 7 -> 0, of which waited for: 3 -> 0; matrix products, arithmetic and copies ran while one was open for 5% -> 0% of each run, Pallas kernels for 0% -> 0%
where the time goes in v1:
time: 91.9 us; the launch traced here: 91.6 us
  Pallas kernels  81.5 us (89%)
  local copies, waits for them, and re-layouts  4.63 us (5%)
  between operations  3.75 us (4%)
  other arithmetic  1.72 us (2%)
    pallas_call x1, Pallas kernels, per_device(): pl.pallas_call(kernel, out_shape=(jax.ShapeDtypeStruct((LON, LATENT), BF1...  81.5 us
    unnamed x6, local copies, waits for them, and re-layouts  3.9 us

profile of v1, /device:TPU:1, one launch (start us, length us, event | category | flops | bytes accessed | tf_op | source)
XLA Modules:
  0.0 91.6 jit_solution(211827247378425921)
XLA Ops:
  1.3 0.7 copy.9
  2.0 0.0 copy-start
  2.0 1.2 %copy-done = bf16[9,100,512]{2,1,0:T(8,128)(2,1)S(1)} copy-done((bf16[9,100,512]{2,1,0:T(8,128)(2,1)S(1)}, bf16[9,100,512]{2,1,0:T(8,128)(2,1)}, u32[]{:S(2)}) %copy-start) | copy-done | bytes 921624
  3.2 0.0 copy-start.1
  3.2 1.1 %copy-done.1 = bf16[1,512,1,720]{1,3,2,0:T(8,128)(2,1)S(1)} copy-done((bf16[1,512,1,720]{1,3,2,0:T(8,128)(2,1)S(1)}, bf16[1,512,1,720]{1,3,2,0:T(8,128)(2,1)}, u32[]{:S(2)}) %copy-start.1) | copy-done | bytes 737304
  4.3 81.5 %decoder.1 = (bf16[720,512]{1,0:T(8,128)(2,1)S(1)}, bf16[2,8,8,16,256]{4,3,2,1,0:T(8,128)(2,1)S(1)}) custom-call(f32[1]{0:T(128)S(6)} %copy.11.area_ref, bf16[720,512]{1,0:T(8,128)(2,1)S(1)} %bitcast.21, bf16[9,100,512]{2,1,0:T(8,128)(2,1)S(1)} %copy-done, f32[48,128]{1,0:T(8,128)S(1)} %pad.4.obs), custom_call_target="tpu_custom_call" | custom-call | flops 2600000000 | bytes 6000000 | tf_op jit(solution)/shard_map/decoder/pallas_call | solution.py:419
  85.8 0.1 slice.31
  85.9 0.5 fusion
  87.7 0.2 convert_multiply_fusion
  87.9 0.1 slice_bitcast_fusion.1
  88.0 1.5 %pad_maximum_fusion = f32[9,100,512]{2,1,0:T(8,128)} fusion(f32[9,100,256]{2,1,0:T(8,128)S(1)} %get-tuple-element.8, f32[9,100,256]{2,1,0:T(8,128)S(1)} %get-tuple-element.7), kind=kLoop, calls=%fused_computation | loop fusion | flops 460800 | bytes 3686400 | tf_op jit(solution)/shard_map/concatenate | solution.py:436
  89.6 0.9 copy.12
  (2 shorter events, 0.0 us)
Async XLA Ops:
  2.0 1.2 %copy-start = (bf16[9,100,512]{2,1,0:T(8,128)(2,1)S(1)}, bf16[9,100,512]{2,1,0:T(8,128)(2,1)}, u32[]{:S(2)}) copy-start(bf16[9,100,512]{2,1,0:T(8,128)(2,1)} %w_ref.1) | copy-start | bytes 2764804
  3.2 1.1 %copy-start.1 = (bf16[1,512,1,720]{1,3,2,0:T(8,128)(2,1)S(1)}, bf16[1,512,1,720]{1,3,2,0:T(8,128)(2,1)}, u32[]{:S(2)}) copy-start(bf16[1,512,1,720]{1,3,2,0:T(8,128)(2,1)} %param.4) | copy-start | bytes 2211844

commit v2 on v1

v2 whole, which is shorter than its diff:
```python
import math

import jax
import jax.numpy as jnp
from jax import lax
from jax.experimental import pallas as pl
from jax.experimental.pallas import tpu as pltpu
from jax.sharding import PartitionSpec as P

MESH = pl.DeviceIdType.MESH
F32 = jnp.float32
BF16 = jnp.bfloat16

CH, LATENT, LON, MEMBERS, NLAT = 100, 512, 720, 16, 32
LANES = 128
BLOCK = LON // MEMBERS
SLOT = 48
RING = 8
HALF = LATENT // 2
SUM_ROWS = 512
SMOOTHING = 0.01
PAIR_COEF = (1.0 - 0.05 / MEMBERS) / (MEMBERS - 1)
TALLY = MEMBERS * NLAT * LON
COLUMNS = (4, 0, 1, 2, 6, 7, 8, 3, 5)
GROUPS = ((3, 4, 5, 0), (1, 2, 6, 7, 8))
SHAPES = ((4, 8), (8, 4))


def remote(src, dst, send_sem, recv_sem, device):
    return pltpu.make_async_remote_copy(
        src_ref=src, dst_ref=dst, send_sem=send_sem, recv_sem=recv_sem,
        device_id=device, device_id_type=MESH,
    )


def far(i, size):
    odd = i % 2
    return size // 2 + (i // 2) * (1 - odd) - ((i + 1) // 2) * odd


def resplit(block):
    total = block[0:1] + block[1:2]
    lead = total.astype(BF16).astype(F32)
    row = lax.broadcasted_iota(jnp.int32, block.shape, 0)
    return jnp.where(row == 0, lead, jnp.where(row == 1, total - lead, block))


class Flow:
    def __init__(self, shape, core, twin, pos, rings, has_loss, dw, bufs, red, sems):
        self.first, self.second = shape
        self.core, self.twin = core, twin
        self.pos, self.rings = pos, rings
        self.has_loss = has_loss
        self.dw, self.red = dw, red
        self.send_c, self.recv_c, self.s1, self.r1, self.s2, self.r2, self.s3, self.r3 = bufs
        self.sems = sems
        self.rows = 16 * self.second

    def copy(self, phase, src, dst, send, recv, device):
        return remote(src, dst, self.sems[2 * phase].at[send], self.sems[2 * phase + 1].at[recv], device)

    def c_copy(self, p):
        return self.copy(0, self.send_c.at[p], self.recv_c.at[p], p, p, self.twin)

    def s1_copy(self, p, slot):
        return self.copy(1, self.s1.at[p], self.r1.at[slot], p, slot, self.rings[0](p))

    def s2_copy(self, p, slot):
        return self.copy(2, self.s2.at[p], self.r2.at[slot], p, slot, self.rings[1](p))

    def s3_copy(self, p, slot):
        return self.copy(3, self.s3, self.r3.at[slot], p, slot, self.rings[2](p))

    def t2_copy(self, p, slot):
        block = self.red.at[self.core, self.pos[0], slot]
        return self.copy(4, block, block, p, slot, self.rings[1](p))

    def t1_copy(self, p, slot):
        block = self.red.at[self.core, slot]
        return self.copy(5, block, block, p, slot, self.rings[0](p))

    def tc_copy(self, half, p):
        block = self.red.at[half, p]
        return self.copy(6, block, block, p, p, self.twin)

    def peers(self, ring, body, near=False):
        size = (self.first, self.second, RING)[ring]

        @pl.loop(0, size - 1)
        def _(i):
            body((self.pos[ring] + far(size - 2 - i if near else i, size)) % size)

    def start(self):
        other = self.dw.at[1 - self.core]
        for p in range(self.first):
            self.send_c[p] = other[p * self.rows:(p + 1) * self.rows, :].astype(BF16)
        self.peers(0, lambda p: self.c_copy(p).start())
        self.c_copy(self.pos[0]).start()

    def chip_sum(self, p):
        self.c_copy(p).wait_recv()
        rows = pl.ds(pl.multiple_of(p * self.rows, self.rows), self.rows)
        total = self.dw[self.core, rows, :] + self.recv_c[p].astype(F32)
        if self.has_loss:
            last = total[self.rows - 16:]
            last = jnp.where(p == self.first - 1, resplit(last), last)
            total = jnp.concatenate([total[:self.rows - 16], last], axis=0)
        return total.astype(BF16)

    def step1(self):
        def send(p):
            self.s1[p] = self.chip_sum(p)
            self.s1_copy(p, self.pos[0]).start()

        self.peers(0, send)
        self.r1[self.pos[0]] = self.chip_sum(self.pos[0])

    def step2(self):
        self.peers(0, lambda p: self.s1_copy(p, p).wait_recv(), near=True)
        total = self.r1[0].astype(F32)
        for p in range(1, self.first):
            total = total + self.r1[p].astype(F32)
        for q in range(self.second):
            block = total[16 * q:16 * (q + 1)]
            if self.has_loss and q == self.second - 1:
                block = jnp.where(self.pos[0] == self.first - 1, resplit(block), block)
            self.s2[q] = block.astype(BF16)
        self.peers(1, lambda p: self.s2_copy(p, self.pos[1]).start())
        self.r2[self.pos[1]] = self.s2[self.pos[1]]

    def special(self, block):
        if not self.has_loss:
            return block
        here = (self.pos[0] == self.first - 1) & (self.pos[1] == self.second - 1)
        return jnp.where(here, resplit(block), block)

    def step3(self):
        self.peers(1, lambda p: self.s2_copy(p, p).wait_recv(), near=True)
        total = self.r2[0].astype(F32)
        for p in range(1, self.second):
            total = total + self.r2[p].astype(F32)
        total = self.special(total).astype(BF16)
        self.s3[...] = total
        self.peers(2, lambda p: self.s3_copy(p, self.pos[2]).start())
        self.r3[self.pos[2]] = total

    def step4(self):
        self.peers(2, lambda p: self.s3_copy(p, p).wait_recv(), near=True)
        total = self.r3[0].astype(F32)
        for p in range(1, RING):
            total = total + self.r3[p].astype(F32)
        self.red[self.core, self.pos[0], self.pos[1]] = self.special(total).astype(BF16)
        self.peers(1, lambda p: self.t2_copy(p, self.pos[1]).start())

    def step5(self):
        self.peers(1, lambda p: self.t2_copy(p, p).wait_recv(), near=True)
        self.peers(0, lambda p: self.t1_copy(p, self.pos[0]).start())
        self.tc_copy(self.core, self.pos[0]).start()

    def step6(self):
        def forward(p):
            self.t1_copy(p, p).wait_recv()
            self.tc_copy(self.core, p).start()

        self.peers(0, forward, near=True)

    def finish(self):
        @pl.loop(0, self.first)
        def _(p):
            self.tc_copy(1 - self.core, p).wait_recv()

        @pl.loop(0, self.first)
        def _(p):
            self.c_copy(p).wait_send()
            self.tc_copy(self.core, p).wait_send()

        def first(p):
            self.s1_copy(p, self.pos[0]).wait_send()
            self.t1_copy(p, self.pos[0]).wait_send()

        def second(p):
            self.s2_copy(p, self.pos[1]).wait_send()
            self.t2_copy(p, self.pos[1]).wait_send()

        self.peers(0, first)
        self.peers(1, second)
        self.peers(2, lambda p: self.s3_copy(p, self.pos[2]).wait_send())


def kernel(area_ref, emb_hbm, w_hbm, obs_hbm, d_ref, red0, red1, *scratch):
    (emb, w_ref, obs_raw, obs, wp, fbuf, pown, ps, pr, send_a, recv_a, vals, send_b, recv_b, hr, gf, gcat,
     dw0, dw1) = scratch[:19]
    bufs = (scratch[19:27], scratch[27:35])
    load, h_send, h_recv, a_send, a_recv, b_send, b_recv, g_send, g_recv = scratch[35:44]
    sums = (scratch[44:58], scratch[58:72])

    me = lax.axis_index("ens")
    row = lax.axis_index("space")
    x_lo, y = me // RING, me % RING
    core = row % 2
    z = (row // 2) % RING
    x_hi = row // (2 * RING)
    x = 2 * x_hi + x_lo
    twin = (me, row + 1 - 2 * core)
    next_row = (row + 2 * core - 1 + NLAT) % NLAT
    other = (me, next_row)
    inner = (row > 0) & (row < NLAT - 1)

    loads = [pltpu.make_async_copy(src, dst, load.at[i])
             for i, (src, dst) in enumerate(((w_hbm, w_ref), (emb_hbm, emb), (obs_hbm, obs_raw)))]
    for copy in loads:
        copy.start()

    def at(x_, y_, z_):
        return ((x_ % 2) * RING + y_, ((x_ // 2) * RING + z_) * 2 + core)

    barrier = pltpu.get_barrier_semaphore()

    def greet(device):
        pl.semaphore_signal(barrier, inc=1, device_id=device, device_id_type=MESH)

    def member(j):
        return ((x_lo + 1 - j % 2) % 2) * RING + (y + far(j // 2, RING)) % RING

    greet(other)
    greet(twin)

    @pl.loop(0, MEMBERS - 1)
    def _(j):
        greet((member(j), row))

    @pl.loop(0, RING - 1)
    def _(i):
        greet(at(x, y, (z + far(i, RING)) % RING))

    greet(at((x + 2) % 4, y, z))
    greet(at((x + 2) % 4 + 1 - 2 * (x % 2), y, z))

    for t in range(9):
        wp[t, 96:, :] = jnp.zeros((LANES - 96, LATENT), BF16)
    fbuf[LON:LON + 16, :] = jnp.zeros((16, LANES), F32)
    obs[...] = jnp.zeros_like(obs)
    loads[0].wait()
    for t in range(9):
        wp[t, 0:CH, :] = w_ref[t]
    loads[1].wait()

    latitude = math.pi * ((row.astype(F32) + 0.5) / NLAT - 0.5)
    east_west = 1.0 / (0.25 + jnp.cos(jnp.full((1, LANES), latitude, F32)))

    def product(first):
        mat = wp[pl.ds(first, 3)].reshape(3 * LANES, LATENT)
        out = lax.dot_general(emb[...], mat, (((1,), (1,)), ((), ())), preferred_element_type=F32)
        return (pltpu.roll(out[:, 0:LANES], 1, 0), out[:, LANES:2 * LANES],
                pltpu.roll(out[:, 2 * LANES:3 * LANES], LON - 1, 0))

    def h_copy(slot, k):
        return remote(ps.at[slot, k], pr.at[slot, k], h_send.at[slot, k], h_recv.at[slot, k], (other, twin)[slot])

    for slot in range(2):
        lower = (1 - core) if slot == 0 else core
        west, mid, east = product(6 * lower)
        fbuf[0:LON, :] = west + mid + east
        for k in range(MEMBERS):
            ps[slot, k] = fbuf[BLOCK * k:BLOCK * k + SLOT, :].astype(BF16)
        if slot == 0:
            pl.semaphore_wait(barrier, MEMBERS - 1 + RING - 1 + 4)

        @pl.loop(0, MEMBERS)
        def _(j):
            h_copy(slot, member(j)).start()

    west, mid, east = product(3)
    fbuf[0:LON, :] = mid + east_west * (west + east)
    for k in range(MEMBERS):
        pown[k] = fbuf[BLOCK * k:BLOCK * k + SLOT, :]

    def a_copy(k, slot):
        return remote(send_a.at[k], recv_a.at[slot], a_send.at[k], a_recv.at[slot], (k, row))

    def forecast(k):
        h_copy(1, k).wait_recv()
        h_copy(0, k).wait_recv()
        total = pown[k] + pr[1, k].astype(F32)
        return (total + jnp.where(inner, pr[0, k].astype(F32), 0.0)).astype(BF16)

    @pl.loop(0, MEMBERS - 1)
    def _(j):
        k = member(j)
        send_a[k] = forecast(k)
        a_copy(k, me).start()

    vals[me] = forecast(me).astype(F32)

    loads[2].wait()
    for i in range(BLOCK):
        obs[i:i + 1, 0:CH] = obs_raw[i]

    @pl.loop(0, MEMBERS - 1)
    def _(j):
        k = member(MEMBERS - 2 - j)
        a_copy(k, k).wait_recv()
        vals[k] = recv_a[k].astype(F32)

    area = area_ref[0]

    def score(j, loss):
        rows = pl.ds(pl.multiple_of(8 * j, 8), 8)
        f = [vals[i, rows, :] for i in range(MEMBERS)]
        o = obs[rows, :]
        grad, pair, total = [], [None] * MEMBERS, None
        pairs = None
        for i in range(MEMBERS):
            d = f[i] - o
            q = d * d + SMOOTHING
            r = lax.rsqrt(q)
            grad.append(d * r)
            total = q * r if total is None else total + q * r
        for i in range(MEMBERS):
            for k in range(i + 1, MEMBERS):
                d = f[i] - f[k]
                q = d * d + SMOOTHING
                r = lax.rsqrt(q)
                u = d * r
                pair[i] = u if pair[i] is None else pair[i] + u
                pair[k] = -u if pair[k] is None else pair[k] - u
                pairs = q * r if pairs is None else pairs + q * r
        for i in range(MEMBERS):
            vals[i, rows, :] = area * (grad[i] - PAIR_COEF * pair[i])
        crps = total - 0.5 * PAIR_COEF * (2.0 * pairs + MEMBERS * math.sqrt(SMOOTHING))
        lon = 8 * j + lax.broadcasted_iota(jnp.int32, (8, LANES), 0)
        ch = lax.broadcasted_iota(jnp.int32, (8, LANES), 1)
        return loss + jnp.where((lon < BLOCK) & (ch < CH), crps, 0.0)

    loss = lax.fori_loop(0, SLOT // 8, score, jnp.zeros((8, LANES), F32))

    def b_copy(k, slot):
        return remote(send_b.at[k], recv_b.at[slot], b_send.at[k], b_recv.at[slot], (k, row))

    @pl.loop(0, MEMBERS - 1)
    def _(j):
        k = member(j)
        send_b[k] = vals[k].astype(BF16)
        b_copy(k, me).start()

    recv_b[me] = vals[me].astype(BF16)

    loss = area * jnp.sum(loss)
    sub = lax.broadcasted_iota(jnp.int32, (16, HALF), 0)
    lead = jnp.full((16, HALF), loss, F32).astype(BF16).astype(F32)
    tail = jnp.where(sub == 0, lead, jnp.where(sub == 1, loss - lead, 0.0))
    for h in range(2):
        dw0[h, CH * len(GROUPS[0]):SUM_ROWS - 16, :] = jnp.zeros((SUM_ROWS - 16 - CH * len(GROUPS[0]), HALF), F32)
        dw0[h, SUM_ROWS - 16:, :] = tail
        dw1[h, CH * len(GROUPS[1]):, :] = jnp.zeros((SUM_ROWS - CH * len(GROUPS[1]), HALF), F32)

    def g_copy(slot, k, device):
        return remote(recv_b.at[k], hr.at[slot, k], g_send.at[slot, k], g_recv.at[slot, k], device)

    g_copy(0, me, other).start()
    g_copy(1, me, twin).start()

    @pl.loop(0, MEMBERS - 1)
    def _(j):
        k = member(MEMBERS - 2 - j)
        b_copy(k, k).wait_recv()
        g_copy(0, k, other).start()
        g_copy(1, k, twin).start()

    def gather(slot, first, block):
        for k in range(MEMBERS):
            gf[slot, 8 + BLOCK * k:8 + BLOCK * k + SLOT, :] = block(k).astype(F32)
        gf[slot, 7:8, :] = gf[slot, LON + 7:LON + 8, :]
        gf[slot, LON + 8:LON + 9, :] = gf[slot, 8:9, :]
        for b in range(3):
            column = COLUMNS.index(first + b) * LANES
            gcat[:, column:column + LANES] = gf[slot, 9 - b:9 - b + LON, :].astype(BF16)

    def outer(t):
        column = COLUMNS.index(t) * LANES
        out = lax.dot_general(gcat[:, column:column + LANES], emb[...], (((0,), (0,)), ((), ())),
                              preferred_element_type=F32)[0:CH]
        if t in (3, 5):
            out = out * east_west[:, 0:1]
        group = 0 if t in GROUPS[0] else 1
        base = GROUPS[group].index(t) * CH
        for h in range(2):
            (dw0, dw1)[group][h, base:base + CH, :] = out[:, HALF * h:HALF * (h + 1)]

    def neighbour(slot, keep):
        @pl.loop(0, MEMBERS)
        def _(k):
            g_copy(slot, k, twin).wait_recv()

        return lambda k: jnp.where(keep, hr[slot, k].astype(F32), 0.0)

    def ring_a(p):
        return at(x, y + (1 - core) * (p - y), z + core * (p - z))

    def ring_b(p):
        return at(x, y + core * (p - y), z + (1 - core) * (p - z))

    def ring_x(p):
        return at(p, y, z)

    pos_a = y + core * (z - y)
    pos_b = z + core * (y - z)
    flows = (
        Flow(SHAPES[0], core, twin, (x, pos_a, pos_b), (ring_x, ring_a, ring_b), True, dw0, bufs[0], red0, sums[0]),
        Flow(SHAPES[1], core, twin, (pos_a, x, pos_b), (ring_a, ring_x, ring_b), False, dw1, bufs[1], red1, sums[1]),
    )

    gather(0, 3, lambda k: recv_b[k])
    for t in (3, 4, 5):
        outer(t)
    gather(1, 0, neighbour(1 - core, row < NLAT - 1))
    outer(0)
    flows[0].start()
    for t in (1, 2):
        outer(t)
    gather(2, 6, neighbour(core, row > 0))
    for t in (6, 7, 8):
        outer(t)
    flows[1].start()
    flows[0].step1()
    flows[1].step1()

    plain = jnp.concatenate([wp[t] for t in COLUMNS[:7]], axis=0)
    scaled = jnp.concatenate([wp[t] for t in COLUMNS[7:]], axis=0)
    moved = jnp.dot(gcat[:, 0:7 * LANES], plain, preferred_element_type=F32)
    moved_ew = jnp.dot(gcat[:, 7 * LANES:], scaled, preferred_element_type=F32)
    d_ref[...] = (moved + east_west[:, 0:1] * moved_ew).astype(BF16)

    for flow in flows:
        flow.step2()
    for flow in flows:
        flow.step3()
    for flow in flows:
        flow.step4()
    for flow in flows:
        flow.step5()
    for flow in flows:
        flow.step6()

    for flow in flows:
        flow.finish()

    @pl.loop(0, MEMBERS)
    def _(k):
        for slot in range(2):
            h_copy(slot, k).wait_send()
            g_copy(slot, k, twin).wait_send()

    @pl.loop(0, MEMBERS - 1)
    def _(j):
        k = member(j)
        a_copy(k, me).wait_send()
        b_copy(k, me).wait_send()


def unpack(d_ref, red0, red1, loss_ref, d_hbm, dw_hbm, buf, out, sem):
    move = pltpu.make_async_copy(d_ref, d_hbm, sem.at[9])
    move.start()
    for g, red in enumerate((red0, red1)):
        for h in range(2):
            buf[g, h] = red[h].reshape(SUM_ROWS, HALF).astype(F32)
    loss_ref[0] = jnp.sum(buf[0, 0, SUM_ROWS - 16:SUM_ROWS - 14, 0:1]) * (1.0 / TALLY)
    copies = []
    for g in range(2):
        for i, t in enumerate(GROUPS[g]):
            for h in range(2):
                out[t, :, HALF * h:HALF * (h + 1)] = buf[g, h, CH * i:CH * (i + 1), :] * (1.0 / TALLY)
            copies.append(pltpu.make_async_copy(out.at[t], dw_hbm.at[t], sem.at[t]))
            copies[-1].start()
    for copy in copies:
        copy.wait()
    move.wait()


def per_device(member_embedding, weights, verifying_observed_grid, area_weight):
    emb = member_embedding[0, :, 0, :].T
    obs = jnp.transpose(verifying_observed_grid, (2, 1, 0))
    vmem = pl.BlockSpec(memory_space=pltpu.VMEM)
    smem = pl.BlockSpec(memory_space=pltpu.SMEM)
    hbm = pl.BlockSpec(memory_space=pltpu.HBM)
    dma = lambda *n: pltpu.SemaphoreType.DMA(n)
    blocks = lambda kind: pltpu.VMEM((MEMBERS, SLOT, LANES), kind)
    scratch = [
        pltpu.VMEM((LON, LATENT), BF16),
        pltpu.VMEM((9, CH, LATENT), BF16),
        pltpu.VMEM((BLOCK, 1, CH), F32),
        pltpu.VMEM((SLOT, LANES), F32),
        pltpu.VMEM((9, LANES, LATENT), BF16),
        pltpu.VMEM((LON + 16, LANES), F32),
        blocks(F32),
        pltpu.VMEM((2, MEMBERS, SLOT, LANES), BF16),
        pltpu.VMEM((2, MEMBERS, SLOT, LANES), BF16),
        blocks(BF16),
        blocks(BF16),
        blocks(F32),
        blocks(BF16),
        blocks(BF16),
        pltpu.VMEM((2, MEMBERS, SLOT, LANES), BF16),
        pltpu.VMEM((3, LON + 32, LANES), F32),
        pltpu.VMEM((LON, 9 * LANES), BF16),
        pltpu.VMEM((2, SUM_ROWS, HALF), F32),
        pltpu.VMEM((2, SUM_ROWS, HALF), F32),
    ]
    for first, second in SHAPES:
        big = pltpu.VMEM((first, 16 * second, HALF), BF16)
        small = pltpu.VMEM((second, 16, HALF), BF16)
        scratch += [big, big, big, big, small, small, pltpu.VMEM((16, HALF), BF16), pltpu.VMEM((RING, 16, HALF), BF16)]
    scratch += [dma(3), dma(2, MEMBERS), dma(2, MEMBERS), dma(MEMBERS), dma(MEMBERS), dma(MEMBERS), dma(MEMBERS),
                dma(2, MEMBERS), dma(2, MEMBERS)]
    for first, second in SHAPES:
        for size in (first, first, second, RING, second, first, first):
            scratch += [dma(size), dma(size)]
    moved, red0, red1 = pl.pallas_call(
        kernel,
        out_shape=(jax.ShapeDtypeStruct((LON, LATENT), BF16),
                   *(jax.ShapeDtypeStruct((2, *shape, 16, HALF), BF16) for shape in SHAPES)),
        in_specs=[smem, hbm, hbm, hbm],
        out_specs=(vmem, vmem, vmem),
        scratch_shapes=scratch,
        compiler_params=pltpu.CompilerParams(
            collective_id=0, has_side_effects=True, vmem_limit_bytes=48 * 1024 * 1024),
        cost_estimate=pl.CostEstimate(flops=2_600_000_000, bytes_accessed=6_000_000, transcendentals=1_000_000),
        name="decoder",
    )(area_weight, *(pltpu.with_memory_space_constraint(a, pltpu.HBM) for a in (emb, weights, obs)))
    loss, moved, grad_weight = pl.pallas_call(
        unpack,
        out_shape=(jax.ShapeDtypeStruct((1,), F32), jax.ShapeDtypeStruct((LON, LATENT), BF16),
                   jax.ShapeDtypeStruct((9, CH, LATENT), F32)),
        in_specs=[vmem, vmem, vmem],
        out_specs=(smem, hbm, hbm),
        scratch_shapes=[pltpu.VMEM((2, 2, SUM_ROWS, HALF), F32), pltpu.VMEM((9, CH, LATENT), F32), dma(10)],
        compiler_params=pltpu.CompilerParams(vmem_limit_bytes=32 * 1024 * 1024),
        cost_estimate=pl.CostEstimate(flops=1_000_000, bytes_accessed=4_500_000, transcendentals=0),
        name="unpack",
    )(moved, red0, red1)
    return loss.reshape(()), moved.T[None, :, None, :], grad_weight


def solution(mesh):
    return jax.shard_map(
        per_device,
        mesh=mesh,
        in_specs=(P("ens", None, "space", None), P(), P(None, "space", "ens"), P("space")),
        out_specs=(P(), P("ens", None, "space", None), P()),
        check_vma=False,
    )
```

time: 91.9 us -> 74.1 us (0.81)
  Pallas kernels: 81.5 us -> 72.7 us
  local copies, waits for them, and re-layouts: 4.63 us -> 0 us
  between operations: 3.75 us -> 1.29 us
  other arithmetic: 1.72 us -> 0 us
    pallas_call x1, Pallas kernels: 81.5 us -> 70.5 us  [per_device(): pl.pallas_call(kernel, out_shape=(jax.ShapeDtypeStruct((LON, LATENT), BF1...]
    unnamed x6 -> x0, local copies, waits for them, and re-layouts: 3.9 us -> none
    pallas_call x0 -> x1, Pallas kernels: none -> 2.17 us  [per_device(): pl.pallas_call(unpack, out_shape=(jax.ShapeDtypeStruct((1,), F32), jax.Sh...]
    concatenate x1 -> x0, other arithmetic: 1.55 us -> none  [per_device(): grad_weight = jnp.concatenate([both[0], both[1]], axis=-1)]
where the time goes in v2:
time: 74.1 us; the launch traced here: 74 us
  Pallas kernels  72.7 us (98%)
  between operations  1.29 us (2%)
    pallas_call x1, Pallas kernels, per_device(): pl.pallas_call(kernel, out_shape=(jax.ShapeDtypeStruct((LON, LATENT), BF1...  70.5 us
    pallas_call x1, Pallas kernels, per_device(): pl.pallas_call(unpack, out_shape=(jax.ShapeDtypeStruct((1,), F32), jax.Sh...  2.17 us

profile of v2, /device:TPU:1, one launch (start us, length us, event | category | flops | bytes accessed | tf_op | source)
XLA Modules:
  0.0 74.0 jit_solution(2281136282582258916)
XLA Ops:
  1.3 70.5 %decoder.1 = (bf16[720,512]{1,0:T(8,128)(2,1)S(1)}, bf16[2,4,8,16,256]{4,3,2,1,0:T(8,128)(2,1)S(1)}, bf16[2,8,4,16,256]{4,3,2,1,0:T(8,128)(2,1)S(1)}) custom-call(f32[1]{0:T(128)S(6)} %copy.7.area_ref, bf16[720,512]{1,0:T(8,128)(2,1)} %bitcast.8, bf16[9,100,512]{2,1,0:T(8,128)(2,1)} %w_hbm.1, f32[45,1,100]{2,1,0:T(1,128)} %bitcast.10), custom_call_target="tpu_custom_call" | custom-call | flops 2600000000 | bytes 6000000 | tf_op jit(solution)/shard_map/decoder/pallas_call | solution.py:518
  71.8 2.2 %unpack.1 = (f32[1]{0:T(128)}, bf16[720,512]{1,0:T(8,128)(2,1)}, f32[9,100,512]{2,1,0:T(8,128)}) custom-call(bf16[720,512]{1,0:T(8,128)(2,1)S(1)} %get-tuple-element.9.d_ref, bf16[2,4,8,16,256]{4,3,2,1,0:T(8,128)(2,1)S(1)} %get-tuple-element.10.red0, bf16[2,8,4,16,256]{4,3,2,1,0:T(8,128)(2,1)S(1)} %get-tuple-element.11.red1), custom_call_target="tpu_custom_call" | custom-call | flops 1000000 | bytes 4500000 | tf_op jit(solution)/shard_map/unpack/pallas_call | solution.py:530

commit v3 on v2

v3 whole, which is shorter than its diff:
```python
import math

import jax
import jax.numpy as jnp
from jax import lax
from jax.experimental import pallas as pl
from jax.experimental.pallas import tpu as pltpu
from jax.sharding import PartitionSpec as P

MESH = pl.DeviceIdType.MESH
F32 = jnp.float32
BF16 = jnp.bfloat16

CH, LATENT, LON, MEMBERS, NLAT = 100, 512, 720, 16, 32
LANES = 128
BLOCK = LON // MEMBERS
SLOT = 48
RING = 8
HALF = LATENT // 2
SUM_ROWS = 512
PIECES = 5
PIECE = LON // PIECES
SMOOTHING = 0.01
PAIR_COEF = (1.0 - 0.05 / MEMBERS) / (MEMBERS - 1)
TALLY = MEMBERS * NLAT * LON
MIDDLE = (4, 3, 5)
UNITS = (((0, 0),), ((0, 1), (1, 0), (1, 1), (2, 0), (2, 1)))
MID_ROWS = 304
SHAPES = ((4, 8), (8, 4))


def steps(first, end):
    return pl.loop(first, end, unroll=True)


def remote(src, dst, send_sem, recv_sem, device):
    return pltpu.make_async_remote_copy(
        src_ref=src, dst_ref=dst, send_sem=send_sem, recv_sem=recv_sem,
        device_id=device, device_id_type=MESH,
    )


def far(i, size):
    odd = i % 2
    return size // 2 + (i // 2) * (1 - odd) - ((i + 1) // 2) * odd


def resplit(block):
    total = block[0:1] + block[1:2]
    lead = total.astype(BF16).astype(F32)
    row = lax.broadcasted_iota(jnp.int32, block.shape, 0)
    return jnp.where(row == 0, lead, jnp.where(row == 1, total - lead, block))


class Flow:
    def __init__(self, shape, pos, rings, has_loss, dw, bufs, sems):
        self.first, self.second = shape
        self.pos, self.rings = pos, rings
        self.has_loss = has_loss
        self.dw = dw
        self.s1, self.r1, self.s2, self.r2 = bufs
        self.sems = sems
        self.rows = 16 * self.second

    def copy(self, phase, src, dst, send, recv, device):
        return remote(src, dst, self.sems[2 * phase].at[send], self.sems[2 * phase + 1].at[recv], device)

    def s1_copy(self, p, slot):
        return self.copy(0, self.s1.at[p], self.r1.at[slot], p, slot, self.rings[0](p))

    def s2_copy(self, p, slot):
        return self.copy(1, self.s2.at[p], self.r2.at[slot], p, slot, self.rings[1](p))

    def peers(self, ring, body, near=False):
        size = (self.first, self.second)[ring]

        @steps(0, size - 1)
        def _(i):
            body((self.pos[ring] + far(size - 2 - i if near else i, size)) % size)

    def step1(self):
        for p in range(self.first):
            self.s1[p] = self.dw[p * self.rows:(p + 1) * self.rows, :].astype(BF16)
        self.peers(0, lambda p: self.s1_copy(p, self.pos[0]).start())
        self.r1[self.pos[0]] = self.s1[self.pos[0]]

    def step2(self):
        self.peers(0, lambda p: self.s1_copy(p, p).wait_recv(), near=True)
        total = self.r1[0].astype(F32)
        for p in range(1, self.first):
            total = total + self.r1[p].astype(F32)
        for q in range(self.second):
            block = total[16 * q:16 * (q + 1)]
            if self.has_loss and q == self.second - 1:
                block = jnp.where(self.pos[0] == self.first - 1, resplit(block), block)
            self.s2[q] = block.astype(BF16)
        self.peers(1, lambda p: self.s2_copy(p, self.pos[1]).start())
        self.r2[self.pos[1]] = self.s2[self.pos[1]]

    def special(self, block):
        if not self.has_loss:
            return block
        here = (self.pos[0] == self.first - 1) & (self.pos[1] == self.second - 1)
        return jnp.where(here, resplit(block), block)

    def step3(self):
        self.peers(1, lambda p: self.s2_copy(p, p).wait_recv(), near=True)
        total = self.r2[0].astype(F32)
        for p in range(1, self.second):
            total = total + self.r2[p].astype(F32)
        return self.special(total).astype(BF16)

    def finish(self):
        self.peers(0, lambda p: self.s1_copy(p, self.pos[0]).wait_send())
        self.peers(1, lambda p: self.s2_copy(p, self.pos[1]).wait_send())


def kernel(area_ref, emb_hbm, w_hbm, obs_hbm, d_ref, red, *scratch):
    (emb, halo, w_ref, obs_raw, obs, wp, fbuf, pown, ps, pr, send_a, recv_a, vals, send_b, recv_b, hr, gf, gcat,
     mid_sum, send_c, recv_c, dw0, dw1) = scratch[:23]
    s3, r3 = scratch[23:25]
    bufs = (scratch[25:29], scratch[29:33])
    (load, h_send, h_recv, e_send, e_recv, a_send, a_recv, b_send, b_recv, g_send, g_recv, c_sem,
     s3_send, s3_recv, ta_send, tx_send, t_recv, tc_send, tc_recv) = scratch[33:52]
    sums = (scratch[52:56], scratch[56:60])

    me = lax.axis_index("ens")
    row = lax.axis_index("space")
    x_lo, y = me // RING, me % RING
    core = row % 2
    z = (row // 2) % RING
    x_hi = row // (2 * RING)
    x = 2 * x_hi + x_lo
    twin = (me, row + 1 - 2 * core)
    next_row = (row + 2 * core - 1 + NLAT) % NLAT
    other = (me, next_row)
    inner = (row > 0) & (row < NLAT - 1)

    order = [3 * ((2 * (1 - core) + i * (1 + core)) % 3) for i in range(3)]
    w_loads = [pltpu.make_async_copy(w_hbm.at[pl.ds(t, 3)], w_ref.at[pl.ds(t, 3)], load.at[i])
               for i, t in enumerate(order)]
    emb_load = pltpu.make_async_copy(emb_hbm, emb, load.at[3])
    obs_load = pltpu.make_async_copy(obs_hbm, obs_raw, load.at[4])
    for copy in (w_loads[0], emb_load, *w_loads[1:], obs_load):
        copy.start()

    def at(x_, y_, z_):
        return ((x_ % 2) * RING + y_, ((x_ // 2) * RING + z_) * 2 + core)

    barrier = pltpu.get_barrier_semaphore()

    def greet(device):
        pl.semaphore_signal(barrier, inc=1, device_id=device, device_id_type=MESH)

    def member(j):
        return ((x_lo + 1 - j % 2) % 2) * RING + (y + far(j // 2, RING)) % RING

    def ring_a(p):
        return at(x, y + (1 - core) * (p - y), z + core * (p - z))

    def ring_b(p):
        return at(x, y + core * (p - y), z + (1 - core) * (p - z))

    def ring_x(p):
        return at(p, y, z)

    pos_a = y + core * (z - y)
    pos_b = z + core * (y - z)

    greet(other)
    greet(twin)

    @steps(0, MEMBERS - 1)
    def _(j):
        greet((member(j), row))

    @steps(0, RING - 1)
    def _(i):
        greet(at(x, y, (z + far(i, RING)) % RING))

    greet(at((x + 2) % 4, y, z))
    greet(at((x + 2) % 4 + 1 - 2 * (x % 2), y, z))
    greetings = MEMBERS - 1 + RING - 1 + 4

    for t in range(9):
        wp[t, 96:, :] = jnp.zeros((LANES - 96, LATENT), BF16)
    fbuf[LON:LON + 16, :] = jnp.zeros((16, LANES), F32)
    obs[...] = jnp.zeros_like(obs)

    def pad(part):
        w_loads[part].wait()
        for i in range(3):
            wp[order[part] + i, 0:CH, :] = w_ref[order[part] + i]

    pad(0)
    emb_load.wait()

    latitude = math.pi * ((row.astype(F32) + 0.5) / NLAT - 0.5)
    east_west = 1.0 / (0.25 + jnp.cos(jnp.full((1, LANES), latitude, F32)))

    def product(first):
        mat = wp[pl.ds(first, 3)].reshape(3 * LANES, LATENT)
        out = lax.dot_general(emb[...], mat, (((1,), (1,)), ((), ())), preferred_element_type=F32)
        return (pltpu.roll(out[:, 0:LANES], 1, 0), out[:, LANES:2 * LANES],
                pltpu.roll(out[:, 2 * LANES:3 * LANES], LON - 1, 0))

    def h_copy(slot, k):
        return remote(ps.at[slot, k], pr.at[slot, k], h_send.at[slot, k], h_recv.at[slot, k], (other, twin)[slot])

    for slot in range(2):
        lower = (1 - core) if slot == 0 else core
        west, mid, east = product(6 * lower)
        pad(slot + 1)
        fbuf[0:LON, :] = west + mid + east
        for k in range(MEMBERS):
            ps[slot, k] = fbuf[BLOCK * k:BLOCK * k + SLOT, :].astype(BF16)
        if slot == 0:
            pl.semaphore_wait(barrier, greetings)

        @steps(0, MEMBERS)
        def _(j):
            h_copy(slot, member(j)).start()

    west, mid, east = product(3)
    fbuf[0:LON, :] = mid + east_west * (west + east)
    for k in range(MEMBERS):
        pown[k] = fbuf[BLOCK * k:BLOCK * k + SLOT, :]

    def a_copy(k, slot):
        return remote(send_a.at[k], recv_a.at[slot], a_send.at[k], a_recv.at[slot], (k, row))

    def forecast(k):
        h_copy(1, k).wait_recv()
        h_copy(0, k).wait_recv()
        total = pown[k] + pr[1, k].astype(F32)
        return (total + jnp.where(inner, pr[0, k].astype(F32), 0.0)).astype(BF16)

    @steps(0, MEMBERS - 1)
    def _(j):
        k = member(j)
        send_a[k] = forecast(k)
        a_copy(k, me).start()

    vals[me] = forecast(me).astype(F32)

    def e_copy(i):
        piece = pl.ds(PIECE * i, PIECE)
        return remote(emb.at[piece], halo.at[piece], e_send.at[i], e_recv.at[i], twin)

    for i in range(PIECES):
        e_copy(i).start()

    obs_load.wait()
    for i in range(BLOCK):
        obs[i:i + 1, 0:CH] = obs_raw[i]

    @steps(0, MEMBERS - 1)
    def _(j):
        k = member(MEMBERS - 2 - j)
        a_copy(k, k).wait_recv()
        vals[k] = recv_a[k].astype(F32)

    area = area_ref[0]

    def score(j, loss):
        rows = pl.ds(pl.multiple_of(8 * j, 8), 8)
        f = [vals[i, rows, :] for i in range(MEMBERS)]
        o = obs[rows, :]
        grad, pair, total = [], [None] * MEMBERS, None
        pairs = None
        for i in range(MEMBERS):
            d = f[i] - o
            q = d * d + SMOOTHING
            r = lax.rsqrt(q)
            grad.append(d * r)
            total = q * r if total is None else total + q * r
        for i in range(MEMBERS):
            for k in range(i + 1, MEMBERS):
                d = f[i] - f[k]
                q = d * d + SMOOTHING
                r = lax.rsqrt(q)
                u = d * r
                pair[i] = u if pair[i] is None else pair[i] + u
                pair[k] = -u if pair[k] is None else pair[k] - u
                pairs = q * r if pairs is None else pairs + q * r
        for i in range(MEMBERS):
            vals[i, rows, :] = area * (grad[i] - PAIR_COEF * pair[i])
        crps = total - 0.5 * PAIR_COEF * (2.0 * pairs + MEMBERS * math.sqrt(SMOOTHING))
        lon = 8 * j + lax.broadcasted_iota(jnp.int32, (8, LANES), 0)
        ch = lax.broadcasted_iota(jnp.int32, (8, LANES), 1)
        return loss + jnp.where((lon < BLOCK) & (ch < CH), crps, 0.0)

    loss = lax.fori_loop(0, SLOT // 8, score, jnp.zeros((8, LANES), F32))

    def b_copy(k, slot):
        return remote(send_b.at[k], recv_b.at[slot], b_send.at[k], b_recv.at[slot], (k, row))

    @steps(0, MEMBERS - 1)
    def _(j):
        k = member(j)
        send_b[k] = vals[k].astype(BF16)
        b_copy(k, me).start()

    recv_b[me] = vals[me].astype(BF16)

    loss = area * jnp.sum(loss)
    sub = lax.broadcasted_iota(jnp.int32, (16, HALF), 0)
    lead = jnp.full((16, HALF), loss, F32).astype(BF16).astype(F32)
    tail = jnp.where(sub == 0, lead, jnp.where(sub == 1, loss - lead, 0.0))
    dw0[4 * CH:SUM_ROWS - 16, :] = jnp.zeros((SUM_ROWS - 16 - 4 * CH, HALF), F32)
    dw0[SUM_ROWS - 16:, :] = tail
    dw1[5 * CH:, :] = jnp.zeros((SUM_ROWS - 5 * CH, HALF), F32)
    for h in range(2):
        mid_sum[h, 3 * CH:, :] = jnp.zeros((MID_ROWS - 3 * CH, HALF), F32)

    def g_copy(slot, k, device):
        return remote(recv_b.at[k], hr.at[slot, k], g_send.at[slot, k], g_recv.at[slot, k], device)

    g_copy(0, me, other).start()
    g_copy(1, me, twin).start()

    @steps(0, MEMBERS - 1)
    def _(j):
        k = member(MEMBERS - 2 - j)
        b_copy(k, k).wait_recv()
        g_copy(0, k, other).start()
        g_copy(1, k, twin).start()

    def gather(slot, columns, block):
        for k in range(MEMBERS):
            gf[slot, 8 + BLOCK * k:8 + BLOCK * k + SLOT, :] = block(k).astype(F32)
        gf[slot, 7:8, :] = gf[slot, LON + 7:LON + 8, :]
        gf[slot, LON + 8:LON + 9, :] = gf[slot, 8:9, :]
        for b, column in enumerate(columns):
            gcat[:, column * LANES:(column + 1) * LANES] = gf[slot, 9 - b:9 - b + LON, :].astype(BF16)

    def arrive(slot):
        @steps(0, MEMBERS)
        def _(k):
            g_copy(slot, k, twin).wait_recv()

    def outer(column, latent):
        return lax.dot_general(gcat[:, column * LANES:(column + 3) * LANES], latent, (((0,), (0,)), ((), ())),
                               preferred_element_type=F32)

    def part(out, i, h):
        return out[LANES * i:LANES * i + CH, HALF * h:HALF * (h + 1)]

    flows = (
        Flow(SHAPES[0], (x, pos_a), (ring_x, ring_a), True, dw0, bufs[0], sums[0]),
        Flow(SHAPES[1], (pos_a, x), (ring_a, ring_x), False, dw1, bufs[1], sums[1]),
    )

    gather(0, (7, 6, 8), lambda k: recv_b[k])
    out = outer(6, emb[...])
    for i in range(3):
        for h in range(2):
            scale = 1.0 if i == 0 else east_west[:, 0:1]
            mid_sum[h, CH * i:CH * (i + 1), :] = part(out, i, h) * scale
    send_c[...] = mid_sum[1 - core].astype(BF16)
    c_copy = remote(send_c, recv_c, c_sem.at[0], c_sem.at[1], twin)
    c_copy.start()
    for i in range(PIECES):
        e_copy(i).wait_recv()
    with_twin = outer(6, halo[...])
    arrive(0)
    gather(1, (0, 1, 2), lambda k: jnp.where(inner, hr[0, k].astype(F32), 0.0))
    across = outer(0, emb[...])
    for group, base in ((1, 0), (0, 3)):
        for n, (b, h) in enumerate(UNITS[group]):
            rows = slice(CH * (base + n), CH * (base + n + 1))
            (dw0, dw1)[group][rows, :] = part(with_twin, (1, 0, 2)[b], h) + part(across, b, h)
    flows[1].step1()
    c_copy.wait_recv()
    dw0[0:3 * CH, :] = (mid_sum[core] + recv_c[...].astype(F32))[0:3 * CH]
    flows[0].step1()

    arrive(1)
    gather(2, (3, 4, 5), lambda k: hr[1, k])
    near = [wp[pl.ds(6 * first, 3)].reshape(3 * LANES, LATENT) for first in (1 - core, core)]
    plain = jnp.concatenate(near + [wp[4]], axis=0)
    scaled = jnp.concatenate([wp[3], wp[5]], axis=0)
    moved = jnp.dot(gcat[:, 0:7 * LANES], plain, preferred_element_type=F32)
    moved_ew = jnp.dot(gcat[:, 7 * LANES:], scaled, preferred_element_type=F32)
    d_ref[...] = (moved + east_west[:, 0:1] * moved_ew).astype(BF16)

    for flow in flows:
        flow.step2()
    for g, flow in enumerate(flows):
        s3[g] = flow.step3()

    def s3_copy(p, slot):
        return remote(s3, r3.at[slot], s3_send.at[p], s3_recv.at[slot], ring_b(p))

    @steps(0, RING - 1)
    def _(i):
        s3_copy((pos_b + far(i, RING)) % RING, pos_b).start()

    r3[pos_b] = s3[...]

    c_copy.wait_send()
    for i in range(PIECES):
        e_copy(i).wait_send()

    @steps(0, MEMBERS)
    def _(k):
        for slot in range(2):
            h_copy(slot, k).wait_send()
            g_copy(slot, k, twin).wait_send()

    @steps(0, MEMBERS - 1)
    def _(j):
        k = member(j)
        a_copy(k, me).wait_send()
        b_copy(k, me).wait_send()

    for flow in flows:
        flow.finish()

    @steps(0, RING - 1)
    def _(i):
        p = (pos_b + far(RING - 2 - i, RING)) % RING
        s3_copy(p, p).wait_recv()

    total = r3[0].astype(F32)
    for p in range(1, RING):
        total = total + r3[p].astype(F32)
    red[core, x, pos_a, 0] = flows[0].special(total[0]).astype(BF16)
    red[core, x, pos_a, 1] = total[1].astype(BF16)

    def ta_copy(i, slot):
        block = red.at[core, x, slot]
        return remote(block, block, ta_send.at[i], t_recv.at[x, slot], ring_a((pos_a + far(i, RING)) % RING))

    def tx_copy(i, x_, slot):
        block = red.at[core, x_, slot]
        return remote(block, block, tx_send.at[slot, i], t_recv.at[x_, slot], ring_x((x + far(i, 4)) % 4))

    def tc_copy(half, x_):
        block = red.at[half, x_]
        return remote(block, block, tc_send.at[x_], tc_recv.at[x_], twin)

    @steps(0, RING - 1)
    def _(i):
        ta_copy(i, pos_a).start()

    def along_x(slot):
        for i in range(3):
            tx_copy(i, x, slot).start()

    along_x(pos_a)

    @steps(0, RING - 1)
    def _(j):
        a_ = (pos_a + far(RING - 2 - j, RING)) % RING
        ta_copy(j, a_).wait_recv()
        along_x(a_)

    tc_copy(core, x).start()

    @steps(0, RING - 1)
    def _(i):
        s3_copy((pos_b + far(i, RING)) % RING, pos_b).wait_send()
        ta_copy(i, pos_a).wait_send()

    @steps(0, 3)
    def _(i):
        x_ = (x + far(2 - i, 4)) % 4
        for j in range(RING):
            tx_copy(i, x_, j).wait_recv()
        tc_copy(core, x_).start()

    @steps(0, RING)
    def _(slot):
        for i in range(3):
            tx_copy(i, x, slot).wait_send()

    @steps(0, 4)
    def _(x_):
        tc_copy(1 - core, x_).wait_recv()

    @steps(0, 4)
    def _(x_):
        tc_copy(core, x_).wait_send()


def unpack(d_ref, red, loss_ref, d_hbm, dw_hbm, buf, out, sem):
    move = pltpu.make_async_copy(d_ref, d_hbm, sem.at[9])
    move.start()
    for h in range(2):
        for x_ in range(4):
            for a_ in range(RING):
                for g, block in enumerate((x_ * RING + a_, a_ * 4 + x_)):
                    buf[g, h, 16 * block:16 * (block + 1), :] = red[h, x_, a_, g].astype(F32)
    tails = buf[0, :, SUM_ROWS - 16:SUM_ROWS - 14, 0:1]
    loss_ref[0] = jnp.sum(tails) * (1.0 / TALLY)

    def unit(t, h, g, core, i):
        out[t, :, HALF * h:HALF * (h + 1)] = buf[g, core, CH * i:CH * (i + 1), :] * (1.0 / TALLY)

    copies = []

    def leave(t):
        copies.append(pltpu.make_async_copy(out.at[t], dw_hbm.at[t], sem.at[t]))
        copies[-1].start()

    for i, t in enumerate(MIDDLE):
        for h in range(2):
            unit(t, h, 0, h, i)
        leave(t)
    for core in range(2):
        for b in range(3):
            for h in range(2):
                group = 0 if (b, h) in UNITS[0] else 1
                unit(6 * (1 - core) + b, h, group, core, (3, 0)[group] + UNITS[group].index((b, h)))
            leave(6 * (1 - core) + b)
    for copy in copies:
        copy.wait()
    move.wait()


def per_device(member_embedding, weights, verifying_observed_grid, area_weight):
    emb = member_embedding[0, :, 0, :].T
    obs = jnp.transpose(verifying_observed_grid, (2, 1, 0))
    vmem = pl.BlockSpec(memory_space=pltpu.VMEM)
    smem = pl.BlockSpec(memory_space=pltpu.SMEM)
    hbm = pl.BlockSpec(memory_space=pltpu.HBM)
    dma = lambda *n: pltpu.SemaphoreType.DMA(n)
    blocks = lambda kind: pltpu.VMEM((MEMBERS, SLOT, LANES), kind)
    scratch = [
        pltpu.VMEM((LON, LATENT), BF16),
        pltpu.VMEM((LON, LATENT), BF16),
        pltpu.VMEM((9, CH, LATENT), BF16),
        pltpu.VMEM((BLOCK, 1, CH), F32),
        pltpu.VMEM((SLOT, LANES), F32),
        pltpu.VMEM((9, LANES, LATENT), BF16),
        pltpu.VMEM((LON + 16, LANES), F32),
        blocks(F32),
        pltpu.VMEM((2, MEMBERS, SLOT, LANES), BF16),
        pltpu.VMEM((2, MEMBERS, SLOT, LANES), BF16),
        blocks(BF16),
        blocks(BF16),
        blocks(F32),
        blocks(BF16),
        blocks(BF16),
        pltpu.VMEM((2, MEMBERS, SLOT, LANES), BF16),
        pltpu.VMEM((3, LON + 32, LANES), F32),
        pltpu.VMEM((LON, 9 * LANES), BF16),
        pltpu.VMEM((2, MID_ROWS, HALF), F32),
        pltpu.VMEM((MID_ROWS, HALF), BF16),
        pltpu.VMEM((MID_ROWS, HALF), BF16),
        pltpu.VMEM((SUM_ROWS, HALF), F32),
        pltpu.VMEM((SUM_ROWS, HALF), F32),
        pltpu.VMEM((2, 16, HALF), BF16),
        pltpu.VMEM((RING, 2, 16, HALF), BF16),
    ]
    for first, second in SHAPES:
        big = pltpu.VMEM((first, 16 * second, HALF), BF16)
        small = pltpu.VMEM((second, 16, HALF), BF16)
        scratch += [big, big, small, small]
    scratch += [dma(5), dma(2, MEMBERS), dma(2, MEMBERS), dma(PIECES), dma(PIECES),
                dma(MEMBERS), dma(MEMBERS), dma(MEMBERS), dma(MEMBERS), dma(2, MEMBERS), dma(2, MEMBERS), dma(2),
                dma(RING), dma(RING), dma(RING), dma(RING, 3), dma(4, RING), dma(4), dma(4)]
    for first, second in SHAPES:
        for size in (first, second):
            scratch += [dma(size), dma(size)]
    moved, red = pl.pallas_call(
        kernel,
        out_shape=(jax.ShapeDtypeStruct((LON, LATENT), BF16),
                   jax.ShapeDtypeStruct((2, 4, RING, 2, 16, HALF), BF16)),
        in_specs=[smem, hbm, hbm, hbm],
        out_specs=(vmem, vmem),
        scratch_shapes=scratch,
        compiler_params=pltpu.CompilerParams(
            collective_id=0, has_side_effects=True, vmem_limit_bytes=48 * 1024 * 1024),
        cost_estimate=pl.CostEstimate(flops=2_600_000_000, bytes_accessed=6_000_000, transcendentals=1_000_000),
        name="decoder",
    )(area_weight, *(pltpu.with_memory_space_constraint(a, pltpu.HBM) for a in (emb, weights, obs)))
    loss, moved, grad_weight = pl.pallas_call(
        unpack,
        out_shape=(jax.ShapeDtypeStruct((1,), F32), jax.ShapeDtypeStruct((LON, LATENT), BF16),
                   jax.ShapeDtypeStruct((9, CH, LATENT), F32)),
        in_specs=[vmem, vmem],
        out_specs=(smem, hbm, hbm),
        scratch_shapes=[pltpu.VMEM((2, 2, SUM_ROWS, HALF), F32), pltpu.VMEM((9, CH, LATENT), F32), dma(10)],
        compiler_params=pltpu.CompilerParams(vmem_limit_bytes=32 * 1024 * 1024),
        cost_estimate=pl.CostEstimate(flops=1_000_000, bytes_accessed=4_500_000, transcendentals=0),
        name="unpack",
    )(moved, red)
    return loss.reshape(()), moved.T[None, :, None, :], grad_weight


def solution(mesh):
    return jax.shard_map(
        per_device,
        mesh=mesh,
        in_specs=(P("ens", None, "space", None), P(), P(None, "space", "ens"), P("space")),
        out_specs=(P(), P("ens", None, "space", None), P()),
        check_vma=False,
    )
```

time: 74.1 us -> 69.4 us (0.937)
  Pallas kernels: 72.7 us -> 68 us
    pallas_call x1, Pallas kernels: 70.5 us -> 65.8 us  [per_device(): pl.pallas_call(kernel, out_shape=(jax.ShapeDtypeStruct((LON, LATENT), BF1...]
where the time goes in v3:
time: 69.4 us; the launch traced here: 69.3 us
  Pallas kernels  68 us (98%)
  between operations  1.29 us (2%)
    pallas_call x1, Pallas kernels, per_device(): pl.pallas_call(kernel, out_shape=(jax.ShapeDtypeStruct((LON, LATENT), BF1...  65.8 us
    pallas_call x1, Pallas kernels, per_device(): pl.pallas_call(unpack, out_shape=(jax.ShapeDtypeStruct((1,), F32), jax.Sh...  2.17 us

profile of v3, /device:TPU:1, one launch (start us, length us, event | category | flops | bytes accessed | tf_op | source)
XLA Modules:
  0.0 69.3 jit_solution(4343362546110693132)
XLA Ops:
  1.3 65.8 %decoder.1 = (bf16[720,512]{1,0:T(8,128)(2,1)S(1)}, bf16[2,4,8,2,16,256]{5,4,3,2,1,0:T(8,128)(2,1)S(1)}) custom-call(f32[1]{0:T(128)S(6)} %copy.7.area_ref, bf16[720,512]{1,0:T(8,128)(2,1)} %bitcast.8, bf16[9,100,512]{2,1,0:T(8,128)(2,1)} %w_hbm.1, f32[45,1,100]{2,1,0:T(1,128)} %bitcast.10), custom_call_target="tpu_custom_call" | custom-call | flops 2600000000 | bytes 6000000 | tf_op jit(solution)/shard_map/decoder/pallas_call | solution.py:567
  67.1 2.2 %unpack.1 = (f32[1]{0:T(128)}, bf16[720,512]{1,0:T(8,128)(2,1)}, f32[9,100,512]{2,1,0:T(8,128)}) custom-call(bf16[720,512]{1,0:T(8,128)(2,1)S(1)} %get-tuple-element.8.d_ref, bf16[2,4,8,2,16,256]{5,4,3,2,1,0:T(8,128)(2,1)S(1)} %get-tuple-element.9.red), custom_call_target="tpu_custom_call" | custom-call | flops 1000000 | bytes 4500000 | tf_op jit(solution)/shard_map/unpack/pallas_call | solution.py:579

commit v4 on v3

--- a/solution.py
+++ b/solution.py
@@ -18,8 +18,6 @@
 RING = 8
 HALF = LATENT // 2
 SUM_ROWS = 512
-PIECES = 5
-PIECE = LON // PIECES
 SMOOTHING = 0.01
 PAIR_COEF = (1.0 - 0.05 / MEMBERS) / (MEMBERS - 1)
 TALLY = MEMBERS * NLAT * LON
@@ -40,9 +38,17 @@
     )
 
 
+def mod(a, n):
+    return a % n if isinstance(a, int) else lax.rem(a, jnp.int32(n))
+
+
+def over(a, n):
+    return a // n if isinstance(a, int) else lax.div(a, jnp.int32(n))
+
+
 def far(i, size):
-    odd = i % 2
-    return size // 2 + (i // 2) * (1 - odd) - ((i + 1) // 2) * odd
+    odd = mod(i, 2)
+    return size // 2 + over(i, 2) * (1 - odd) - over(i + 1, 2) * odd
 
 
 def resplit(block):
@@ -76,7 +82,7 @@
 
         @steps(0, size - 1)
         def _(i):
-            body((self.pos[ring] + far(size - 2 - i if near else i, size)) % size)
+            body(mod(self.pos[ring] + far(size - 2 - i if near else i, size), size))
 
     def step1(self):
         for p in range(self.first):
@@ -118,25 +124,25 @@
 def kernel(area_ref, emb_hbm, w_hbm, obs_hbm, d_ref, red, *scratch):
     (emb, halo, w_ref, obs_raw, obs, wp, fbuf, pown, ps, pr, send_a, recv_a, vals, send_b, recv_b, hr, gf, gcat,
      mid_sum, send_c, recv_c, dw0, dw1) = scratch[:23]
-    s3, r3 = scratch[23:25]
-    bufs = (scratch[25:29], scratch[29:33])
-    (load, h_send, h_recv, e_send, e_recv, a_send, a_recv, b_send, b_recv, g_send, g_recv, c_sem,
-     s3_send, s3_recv, ta_send, tx_send, t_recv, tc_send, tc_recv) = scratch[33:52]
-    sums = (scratch[52:56], scratch[56:60])
+    s3, r3, waits = scratch[23:26]
+    bufs = (scratch[26:30], scratch[30:34])
+    (load, h_send, h_recv, e_sem, a_send, a_recv, b_send, b_recv, g_send, g_recv, c_sem,
+     s3_send, s3_recv, t_send, t_recv, tc_send, tc_recv) = scratch[34:51]
+    sums = (scratch[51:55], scratch[55:59])
 
     me = lax.axis_index("ens")
     row = lax.axis_index("space")
-    x_lo, y = me // RING, me % RING
-    core = row % 2
-    z = (row // 2) % RING
-    x_hi = row // (2 * RING)
+    x_lo, y = over(me, RING), mod(me, RING)
+    core = mod(row, 2)
+    z = mod(over(row, 2), RING)
+    x_hi = over(row, 2 * RING)
     x = 2 * x_hi + x_lo
     twin = (me, row + 1 - 2 * core)
-    next_row = (row + 2 * core - 1 + NLAT) % NLAT
+    next_row = mod(row + 2 * core - 1 + NLAT, NLAT)
     other = (me, next_row)
     inner = (row > 0) & (row < NLAT - 1)
 
-    order = [3 * ((2 * (1 - core) + i * (1 + core)) % 3) for i in range(3)]
+    order = [3 * mod(2 * (1 - core) + i * (1 + core), 3) for i in range(3)]
     w_loads = [pltpu.make_async_copy(w_hbm.at[pl.ds(t, 3)], w_ref.at[pl.ds(t, 3)], load.at[i])
                for i, t in enumerate(order)]
     emb_load = pltpu.make_async_copy(emb_hbm, emb, load.at[3])
@@ -145,7 +151,7 @@
         copy.start()
 
     def at(x_, y_, z_):
-        return ((x_ % 2) * RING + y_, ((x_ // 2) * RING + z_) * 2 + core)
+        return (mod(x_, 2) * RING + y_, (over(x_, 2) * RING + z_) * 2 + core)
 
     barrier = pltpu.get_barrier_semaphore()
 
@@ -153,7 +159,7 @@
         pl.semaphore_signal(barrier, inc=1, device_id=device, device_id_type=MESH)
 
     def member(j):
-        return ((x_lo + 1 - j % 2) % 2) * RING + (y + far(j // 2, RING)) % RING
+        return mod(x_lo + 1 - mod(j, 2), 2) * RING + mod(y + far(over(j, 2), RING), RING)
 
     def ring_a(p):
         return at(x, y + (1 - core) * (p - y), z + core * (p - z))
@@ -176,10 +182,10 @@
 
     @steps(0, RING - 1)
     def _(i):
-        greet(at(x, y, (z + far(i, RING)) % RING))
-
-    greet(at((x + 2) % 4, y, z))
-    greet(at((x + 2) % 4 + 1 - 2 * (x % 2), y, z))
+        greet(at(x, y, mod(z + far(i, RING), RING)))
+
+    greet(at(mod(x + 2, 4), y, z))
+    greet(at(mod(x + 2, 4) + 1 - 2 * mod(x, 2), y, z))
     greetings = MEMBERS - 1 + RING - 1 + 4
 
     for t in range(9):
@@ -204,8 +210,10 @@
         return (pltpu.roll(out[:, 0:LANES], 1, 0), out[:, LANES:2 * LANES],
                 pltpu.roll(out[:, 2 * LANES:3 * LANES], LON - 1, 0))
 
-    def h_copy(slot, k):
-        return remote(ps.at[slot, k], pr.at[slot, k], h_send.at[slot, k], h_recv.at[slot, k], (other, twin)[slot])
+    def h_copy(k):
+        return remote(ps.at[0, k], pr.at[0, k], h_send.at[k], h_recv.at[k], other)
+
+    h_twin = remote(ps.at[1], pr.at[1], h_send.at[MEMBERS], h_recv.at[MEMBERS], twin)
 
     for slot in range(2):
         lower = (1 - core) if slot == 0 else core
@@ -214,12 +222,14 @@
         fbuf[0:LON, :] = west + mid + east
         for k in range(MEMBERS):
             ps[slot, k] = fbuf[BLOCK * k:BLOCK * k + SLOT, :].astype(BF16)
-        if slot == 0:
-            pl.semaphore_wait(barrier, greetings)
+        if slot == 1:
+            h_twin.start()
+            continue
+        pl.semaphore_wait(barrier, greetings)
 
         @steps(0, MEMBERS)
         def _(j):
-            h_copy(slot, member(j)).start()
+            h_copy(member(j)).start()
 
     west, mid, east = product(3)
     fbuf[0:LON, :] = mid + east_west * (west + east)
@@ -230,10 +240,11 @@
         return remote(send_a.at[k], recv_a.at[slot], a_send.at[k], a_recv.at[slot], (k, row))
 
     def forecast(k):
-        h_copy(1, k).wait_recv()
-        h_copy(0, k).wait_recv()
+        h_copy(k).wait_recv()
         total = pown[k] + pr[1, k].astype(F32)
         return (total + jnp.where(inner, pr[0, k].astype(F32), 0.0)).astype(BF16)
+
+    h_twin.wait_recv()
 
     @steps(0, MEMBERS - 1)
     def _(j):
@@ -243,12 +254,8 @@
 
     vals[me] = forecast(me).astype(F32)
 
-    def e_copy(i):
-        piece = pl.ds(PIECE * i, PIECE)
-        return remote(emb.at[piece], halo.at[piece], e_send.at[i], e_recv.at[i], twin)
-
-    for i in range(PIECES):
-        e_copy(i).start()
+    e_copy = remote(emb, halo, e_sem.at[0], e_sem.at[1], twin)
+    e_copy.start()
 
     obs_load.wait()
     for i in range(BLOCK):
@@ -313,18 +320,19 @@
     for h in range(2):
         mid_sum[h, 3 * CH:, :] = jnp.zeros((MID_ROWS - 3 * CH, HALF), F32)
 
-    def g_copy(slot, k, device):
-        return remote(recv_b.at[k], hr.at[slot, k], g_send.at[slot, k], g_recv.at[slot, k], device)
-
-    g_copy(0, me, other).start()
-    g_copy(1, me, twin).start()
+    def g_copy(k):
+        return remote(recv_b.at[k], hr.at[0, k], g_send.at[k], g_recv.at[k], other)
+
+    g_copy(me).start()
 
     @steps(0, MEMBERS - 1)
     def _(j):
         k = member(MEMBERS - 2 - j)
         b_copy(k, k).wait_recv()
-        g_copy(0, k, other).start()
-        g_copy(1, k, twin).start()
+        g_copy(k).start()
+
+    g_twin = remote(recv_b, hr.at[1], g_send.at[MEMBERS], g_recv.at[MEMBERS], twin)
+    g_twin.start()
 
     def gather(slot, columns, block):
         for k in range(MEMBERS):
@@ -333,11 +341,6 @@
         gf[slot, LON + 8:LON + 9, :] = gf[slot, 8:9, :]
         for b, column in enumerate(columns):
             gcat[:, column * LANES:(column + 1) * LANES] = gf[slot, 9 - b:9 - b + LON, :].astype(BF16)
-
-    def arrive(slot):
-        @steps(0, MEMBERS)
-        def _(k):
-            g_copy(slot, k, twin).wait_recv()
 
     def outer(column, latent):
         return lax.dot_general(gcat[:, column * LANES:(column + 3) * LANES], latent, (((0,), (0,)), ((), ())),
@@ -360,10 +363,13 @@
     send_c[...] = mid_sum[1 - core].astype(BF16)
     c_copy = remote(send_c, recv_c, c_sem.at[0], c_sem.at[1], twin)
     c_copy.start()
-    for i in range(PIECES):
-        e_copy(i).wait_recv()
+    e_copy.wait_recv()
     with_twin = outer(6, halo[...])
-    arrive(0)
+
+    @steps(0, MEMBERS)
+    def _(k):
+        g_copy(k).wait_recv()
+
     gather(1, (0, 1, 2), lambda k: jnp.where(inner, hr[0, k].astype(F32), 0.0))
     across = outer(0, emb[...])
     for group, base in ((1, 0), (0, 3)):
@@ -375,7 +381,7 @@
     dw0[0:3 * CH, :] = (mid_sum[core] + recv_c[...].astype(F32))[0:3 * CH]
     flows[0].step1()
 
-    arrive(1)
+    g_twin.wait_recv()
     gather(2, (3, 4, 5), lambda k: hr[1, k])
     near = [wp[pl.ds(6 * first, 3)].reshape(3 * LANES, LATENT) for first in (1 - core, core)]
     plain = jnp.concatenate(near + [wp[4]], axis=0)
@@ -394,19 +400,19 @@
 
     @steps(0, RING - 1)
     def _(i):
-        s3_copy((pos_b + far(i, RING)) % RING, pos_b).start()
+        s3_copy(mod(pos_b + far(i, RING), RING), pos_b).start()
 
     r3[pos_b] = s3[...]
 
     c_copy.wait_send()
-    for i in range(PIECES):
-        e_copy(i).wait_send()
+    e_copy.wait_send()
+    h_twin.wait_send()
+    g_twin.wait_send()
 
     @steps(0, MEMBERS)
     def _(k):
-        for slot in range(2):
-            h_copy(slot, k).wait_send()
-            g_copy(slot, k, twin).wait_send()
+        h_copy(k).wait_send()
+        g_copy(k).wait_send()
 
     @steps(0, MEMBERS - 1)
     def _(j):
@@ -419,7 +425,7 @@
 
     @steps(0, RING - 1)
     def _(i):
-        p = (pos_b + far(RING - 2 - i, RING)) % RING
+        p = mod(pos_b + far(RING - 2 - i, RING), RING)
         s3_copy(p, p).wait_recv()
 
     total = r3[0].astype(F32)
@@ -428,52 +434,82 @@
     red[core, x, pos_a, 0] = flows[0].special(total[0]).astype(BF16)
     red[core, x, pos_a, 1] = total[1].astype(BF16)
 
-    def ta_copy(i, slot):
-        block = red.at[core, x, slot]
-        return remote(block, block, ta_send.at[i], t_recv.at[x, slot], ring_a((pos_a + far(i, RING)) % RING))
-
-    def tx_copy(i, x_, slot):
-        block = red.at[core, x_, slot]
-        return remote(block, block, tx_send.at[slot, i], t_recv.at[x_, slot], ring_x((x + far(i, 4)) % 4))
+    def ta_copy(g, x_, i):
+        block = red.at[core, x_, pos_a, g]
+        return remote(block, block, t_send.at[g], t_recv.at[x_, pos_a, g], ring_a(mod(pos_a + far(i, RING), RING)))
+
+    def tx_copy(g, slot, i):
+        block = red.at[core, x, slot, g]
+        return remote(block, block, t_send.at[2 + g], t_recv.at[x, slot, g], ring_x(mod(x + far(i, 4), 4)))
+
+    def along_x(g, slot):
+        for i in range(3):
+            tx_copy(g, slot, i).start()
+
+    def along_ring(g, x_):
+        for i in range(RING - 1):
+            ta_copy(g, x_, i).start()
+
+    def landed(x_, slot, g):
+        block = red.at[core, x_, slot, g]
+        remote(block, block, t_send.at[0], t_recv.at[x_, slot, g], twin).wait_recv()
+
+    def left(sem, blocks, like):
+        part = like.at[pl.ds(0, blocks)]
+        pltpu.make_async_copy(part, part, t_send.at[sem]).wait()
 
     def tc_copy(half, x_):
         block = red.at[half, x_]
         return remote(block, block, tc_send.at[x_], tc_recv.at[x_], twin)
 
+    along_x(1, pos_a)
+    along_ring(0, x)
+    along_x(0, pos_a)
+    along_ring(1, x)
+
+    def from_ring(*offsets):
+        for offset in offsets:
+            slot = mod(pos_a + offset, RING)
+            landed(x, slot, 0)
+            along_x(0, slot)
+
+    def from_x(*offsets):
+        for offset in offsets:
+            x_ = mod(x + offset, 4)
+            landed(x_, pos_a, 1)
+            along_ring(1, x_)
+
+    from_ring(1, 7)
+    from_x(1, 3)
+    from_ring(2, 6)
+    from_x(2)
+    from_ring(3, 5, 4)
+
+    @steps(1, RING)
+    def _(i):
+        landed(x, mod(pos_a + i, RING), 1)
+
+    tc_copy(core, x).start()
+
     @steps(0, RING - 1)
     def _(i):
-        ta_copy(i, pos_a).start()
-
-    def along_x(slot):
-        for i in range(3):
-            tx_copy(i, x, slot).start()
-
-    along_x(pos_a)
-
-    @steps(0, RING - 1)
-    def _(j):
-        a_ = (pos_a + far(RING - 2 - j, RING)) % RING
-        ta_copy(j, a_).wait_recv()
-        along_x(a_)
-
-    tc_copy(core, x).start()
-
-    @steps(0, RING - 1)
-    def _(i):
-        s3_copy((pos_b + far(i, RING)) % RING, pos_b).wait_send()
-        ta_copy(i, pos_a).wait_send()
-
-    @steps(0, 3)
-    def _(i):
-        x_ = (x + far(2 - i, 4)) % 4
-        for j in range(RING):
-            tx_copy(i, x_, j).wait_recv()
+        s3_copy(mod(pos_b + far(i, RING), RING), pos_b).wait_send()
+
+    for offset in (1, 3, 2):
+        x_ = mod(x + offset, 4)
+        landed(x_, pos_a, 0)
+
+        @steps(1, RING)
+        def _(i):
+            for g in range(2):
+                landed(x_, mod(pos_a + i, RING), g)
+
         tc_copy(core, x_).start()
 
-    @steps(0, RING)
-    def _(slot):
-        for i in range(3):
-            tx_copy(i, x, slot).wait_send()
+    left(0, RING - 1, flows[0].s2)
+    left(1, 4 * (RING - 1), waits)
+    left(2, 3 * RING, waits)
+    left(3, 3, flows[0].s2)
 
     @steps(0, 4)
     def _(x_):
@@ -553,14 +589,15 @@
         pltpu.VMEM((SUM_ROWS, HALF), F32),
         pltpu.VMEM((2, 16, HALF), BF16),
         pltpu.VMEM((RING, 2, 16, HALF), BF16),
+        pltpu.VMEM((4 * RING, 16, HALF), BF16),
     ]
     for first, second in SHAPES:
         big = pltpu.VMEM((first, 16 * second, HALF), BF16)
         small = pltpu.VMEM((second, 16, HALF), BF16)
         scratch += [big, big, small, small]
-    scratch += [dma(5), dma(2, MEMBERS), dma(2, MEMBERS), dma(PIECES), dma(PIECES),
-                dma(MEMBERS), dma(MEMBERS), dma(MEMBERS), dma(MEMBERS), dma(2, MEMBERS), dma(2, MEMBERS), dma(2),
-                dma(RING), dma(RING), dma(RING), dma(RING, 3), dma(4, RING), dma(4), dma(4)]
+    scratch += [dma(5), dma(MEMBERS + 1), dma(MEMBERS + 1), dma(2),
+                dma(MEMBERS), dma(MEMBERS), dma(MEMBERS), dma(MEMBERS), dma(MEMBERS + 1), dma(MEMBERS + 1), dma(2),
+                dma(RING), dma(RING), dma(4), dma(4, RING, 2), dma(4), dma(4)]
     for first, second in SHAPES:
         for size in (first, second):
             scratch += [dma(size), dma(size)]

time: 69.4 us -> 68.6 us (0.988)
  Pallas kernels: 68 us -> 67.2 us
    pallas_call x1, Pallas kernels: 65.8 us -> 65 us  [per_device(): pl.pallas_call(kernel, out_shape=(jax.ShapeDtypeStruct((LON, LATENT), BF1...]
where the time goes in v4:
time: 68.6 us; the launch traced here: 68.5 us
  Pallas kernels  67.2 us (98%)
  between operations  1.29 us (2%)
    pallas_call x1, Pallas kernels, per_device(): pl.pallas_call(kernel, out_shape=(jax.ShapeDtypeStruct((LON, LATENT), BF1...  65 us
    pallas_call x1, Pallas kernels, per_device(): pl.pallas_call(unpack, out_shape=(jax.ShapeDtypeStruct((1,), F32), jax.Sh...  2.17 us

profile of v4, /device:TPU:1, one launch (start us, length us, event | category | flops | bytes accessed | tf_op | source)
XLA Modules:
  0.0 68.5 jit_solution(2522349822775517216)
XLA Ops:
  1.3 65.0 %decoder.1 = (bf16[720,512]{1,0:T(8,128)(2,1)S(1)}, bf16[2,4,8,2,16,256]{5,4,3,2,1,0:T(8,128)(2,1)S(1)}) custom-call(f32[1]{0:T(128)S(6)} %copy.7.area_ref, bf16[720,512]{1,0:T(8,128)(2,1)} %bitcast.8, bf16[9,100,512]{2,1,0:T(8,128)(2,1)} %w_hbm.1, f32[45,1,100]{2,1,0:T(1,128)} %bitcast.10), custom_call_target="tpu_custom_call" | custom-call | flops 2600000000 | bytes 6000000 | tf_op jit(solution)/shard_map/decoder/pallas_call | solution.py:604
  66.3 2.2 %unpack.1 = (f32[1]{0:T(128)}, bf16[720,512]{1,0:T(8,128)(2,1)}, f32[9,100,512]{2,1,0:T(8,128)}) custom-call(bf16[720,512]{1,0:T(8,128)(2,1)S(1)} %get-tuple-element.8.d_ref, bf16[2,4,8,2,16,256]{5,4,3,2,1,0:T(8,128)(2,1)S(1)} %get-tuple-element.9.red), custom_call_target="tpu_custom_call" | custom-call | flops 1000000 | bytes 4500000 | tf_op jit(solution)/shard_map/unpack/pallas_call | solution.py:616

commit v5 on v4

--- a/solution.py
+++ b/solution.py
@@ -267,7 +267,7 @@
         a_copy(k, k).wait_recv()
         vals[k] = recv_a[k].astype(F32)
 
-    area = area_ref[0]
+    area = area_ref[...]
 
     def score(j, loss):
         rows = pl.ds(pl.multiple_of(8 * j, 8), 8)
@@ -310,7 +310,7 @@
 
     recv_b[me] = vals[me].astype(BF16)
 
-    loss = area * jnp.sum(loss)
+    loss = jnp.sum(area * loss)
     sub = lax.broadcasted_iota(jnp.int32, (16, HALF), 0)
     lead = jnp.full((16, HALF), loss, F32).astype(BF16).astype(F32)
     tail = jnp.where(sub == 0, lead, jnp.where(sub == 1, loss - lead, 0.0))
@@ -520,7 +520,7 @@
         tc_copy(core, x_).wait_send()
 
 
-def unpack(d_ref, red, loss_ref, d_hbm, dw_hbm, buf, out, sem):
+def unpack(d_ref, red, loss_hbm, d_hbm, dw_hbm, buf, out, loss_ref, sem):
     move = pltpu.make_async_copy(d_ref, d_hbm, sem.at[9])
     move.start()
     for h in range(2):
@@ -528,13 +528,13 @@
             for a_ in range(RING):
                 for g, block in enumerate((x_ * RING + a_, a_ * 4 + x_)):
                     buf[g, h, 16 * block:16 * (block + 1), :] = red[h, x_, a_, g].astype(F32)
-    tails = buf[0, :, SUM_ROWS - 16:SUM_ROWS - 14, 0:1]
-    loss_ref[0] = jnp.sum(tails) * (1.0 / TALLY)
+    tails = jnp.concatenate([buf[0, h, SUM_ROWS - 16:SUM_ROWS - 14, 0:1] for h in range(2)], axis=0)
+    loss_ref[...] = jnp.sum(tails, axis=0, keepdims=True) * (1.0 / TALLY)
+    copies = [pltpu.make_async_copy(loss_ref, loss_hbm, sem.at[10])]
+    copies[0].start()
 
     def unit(t, h, g, core, i):
         out[t, :, HALF * h:HALF * (h + 1)] = buf[g, core, CH * i:CH * (i + 1), :] * (1.0 / TALLY)
-
-    copies = []
 
     def leave(t):
         copies.append(pltpu.make_async_copy(out.at[t], dw_hbm.at[t], sem.at[t]))
@@ -559,7 +559,6 @@
     emb = member_embedding[0, :, 0, :].T
     obs = jnp.transpose(verifying_observed_grid, (2, 1, 0))
     vmem = pl.BlockSpec(memory_space=pltpu.VMEM)
-    smem = pl.BlockSpec(memory_space=pltpu.SMEM)
     hbm = pl.BlockSpec(memory_space=pltpu.HBM)
     dma = lambda *n: pltpu.SemaphoreType.DMA(n)
     blocks = lambda kind: pltpu.VMEM((MEMBERS, SLOT, LANES), kind)
@@ -605,21 +604,22 @@
         kernel,
         out_shape=(jax.ShapeDtypeStruct((LON, LATENT), BF16),
                    jax.ShapeDtypeStruct((2, 4, RING, 2, 16, HALF), BF16)),
-        in_specs=[smem, hbm, hbm, hbm],
+        in_specs=[vmem, hbm, hbm, hbm],
         out_specs=(vmem, vmem),
         scratch_shapes=scratch,
         compiler_params=pltpu.CompilerParams(
             collective_id=0, has_side_effects=True, vmem_limit_bytes=48 * 1024 * 1024),
         cost_estimate=pl.CostEstimate(flops=2_600_000_000, bytes_accessed=6_000_000, transcendentals=1_000_000),
         name="decoder",
-    )(area_weight, *(pltpu.with_memory_space_constraint(a, pltpu.HBM) for a in (emb, weights, obs)))
+    )(jnp.broadcast_to(area_weight, (8, LANES)), *(pltpu.with_memory_space_constraint(a, pltpu.HBM) for a in (emb, weights, obs)))
     loss, moved, grad_weight = pl.pallas_call(
         unpack,
-        out_shape=(jax.ShapeDtypeStruct((1,), F32), jax.ShapeDtypeStruct((LON, LATENT), BF16),
+        out_shape=(jax.ShapeDtypeStruct((1, 1), F32), jax.ShapeDtypeStruct((LON, LATENT), BF16),
                    jax.ShapeDtypeStruct((9, CH, LATENT), F32)),
         in_specs=[vmem, vmem],
-        out_specs=(smem, hbm, hbm),
-        scratch_shapes=[pltpu.VMEM((2, 2, SUM_ROWS, HALF), F32), pltpu.VMEM((9, CH, LATENT), F32), dma(10)],
+        out_specs=(hbm, hbm, hbm),
+        scratch_shapes=[pltpu.VMEM((2, 2, SUM_ROWS, HALF), F32), pltpu.VMEM((9, CH, LATENT), F32),
+                        pltpu.VMEM((1, 1), F32), dma(11)],
         compiler_params=pltpu.CompilerParams(vmem_limit_bytes=32 * 1024 * 1024),
         cost_estimate=pl.CostEstimate(flops=1_000_000, bytes_accessed=4_500_000, transcendentals=0),
         name="unpack",

time: 68.6 us -> 67.6 us (0.985)
  Pallas kernels: 67.2 us -> 66.2 us
where the time goes in v5:
time: 67.6 us; the launch traced here: 67.5 us
  Pallas kernels  66.2 us (98%)
  between operations  1.29 us (2%)
    pallas_call x1, Pallas kernels, per_device(): pl.pallas_call(kernel, out_shape=(jax.ShapeDtypeStruct((LON, LATENT), BF1...  64.6 us
    pallas_call x1, Pallas kernels, per_device(): pl.pallas_call(unpack, out_shape=(jax.ShapeDtypeStruct((1, 1), F32), jax....  1.59 us

profile of v5, /device:TPU:1, one launch (start us, length us, event | category | flops | bytes accessed | tf_op | source)
XLA Modules:
  0.0 67.5 jit_solution(14445422892703487546)
XLA Ops:
  1.3 64.6 %decoder.1 = (bf16[720,512]{1,0:T(8,128)(2,1)S(1)}, bf16[2,4,8,2,16,256]{5,4,3,2,1,0:T(8,128)(2,1)S(1)}) custom-call(f32[8,128]{1,0:T(8,128)S(1)} %broadcast_in_dim.8.area_ref, bf16[720,512]{1,0:T(8,128)(2,1)} %bitcast.10, bf16[9,100,512]{2,1,0:T(8,128)(2,1)} %w_hbm.1, f32[45,1,100]{2,1,0:T(1,128)} %bitcast.12), custom_call_target="tpu_custom_call" | custom-call | flops 2600000000 | bytes 6000000 | tf_op jit(solution)/shard_map/decoder/pallas_call | solution.py:603
  65.9 1.6 %unpack.1 = (f32[1,1]{1,0:T(1,128)}, bf16[720,512]{1,0:T(8,128)(2,1)}, f32[9,100,512]{2,1,0:T(8,128)}) custom-call(bf16[720,512]{1,0:T(8,128)(2,1)S(1)} %get-tuple-element.8.d_ref, bf16[2,4,8,2,16,256]{5,4,3,2,1,0:T(8,128)(2,1)S(1)} %get-tuple-element.9.red), custom_call_target="tpu_custom_call" | custom-call | flops 1000000 | bytes 4500000 | tf_op jit(solution)/shard_map/unpack/pallas_call | solution.py:615
  (1 shorter events, 0.0 us)

commit v6 on v5

--- a/solution.py
+++ b/solution.py
@@ -434,25 +434,16 @@
     red[core, x, pos_a, 0] = flows[0].special(total[0]).astype(BF16)
     red[core, x, pos_a, 1] = total[1].astype(BF16)
 
-    def ta_copy(g, x_, i):
-        block = red.at[core, x_, pos_a, g]
-        return remote(block, block, t_send.at[g], t_recv.at[x_, pos_a, g], ring_a(mod(pos_a + far(i, RING), RING)))
-
-    def tx_copy(g, slot, i):
-        block = red.at[core, x, slot, g]
-        return remote(block, block, t_send.at[2 + g], t_recv.at[x, slot, g], ring_x(mod(x + far(i, 4), 4)))
-
-    def along_x(g, slot):
+    def along_x(block, send, recv):
         for i in range(3):
-            tx_copy(g, slot, i).start()
-
-    def along_ring(g, x_):
+            remote(block, block, t_send.at[send], recv, ring_x(mod(x + far(i, 4), 4))).start()
+
+    def along_ring(block, send, recv):
         for i in range(RING - 1):
-            ta_copy(g, x_, i).start()
-
-    def landed(x_, slot, g):
-        block = red.at[core, x_, slot, g]
-        remote(block, block, t_send.at[0], t_recv.at[x_, slot, g], twin).wait_recv()
+            remote(block, block, t_send.at[send], recv, ring_a(mod(pos_a + far(i, RING), RING))).start()
+
+    def landed(block, recv):
+        remote(block, block, t_send.at[0], recv, twin).wait_recv()
 
     def left(sem, blocks, like):
         part = like.at[pl.ds(0, blocks)]
@@ -462,22 +453,20 @@
         block = red.at[half, x_]
         return remote(block, block, tc_send.at[x_], tc_recv.at[x_], twin)
 
-    along_x(1, pos_a)
-    along_ring(0, x)
-    along_x(0, pos_a)
-    along_ring(1, x)
+    along_x(red.at[core, x, pos_a], 3, t_recv.at[x, pos_a, 0])
+    along_ring(red.at[core, x, pos_a], 0, t_recv.at[x, pos_a, 0])
 
     def from_ring(*offsets):
         for offset in offsets:
             slot = mod(pos_a + offset, RING)
-            landed(x, slot, 0)
-            along_x(0, slot)
+            landed(red.at[core, x, slot], t_recv.at[x, slot, 0])
+            along_x(red.at[core, x, slot, 0], 2, t_recv.at[x, slot, 0])
 
     def from_x(*offsets):
         for offset in offsets:
             x_ = mod(x + offset, 4)
-            landed(x_, pos_a, 1)
-            along_ring(1, x_)
+            landed(red.at[core, x_, pos_a], t_recv.at[x_, pos_a, 0])
+            along_ring(red.at[core, x_, pos_a, 1], 1, t_recv.at[x_, pos_a, 1])
 
     from_ring(1, 7)
     from_x(1, 3)
@@ -485,10 +474,6 @@
     from_x(2)
     from_ring(3, 5, 4)
 
-    @steps(1, RING)
-    def _(i):
-        landed(x, mod(pos_a + i, RING), 1)
-
     tc_copy(core, x).start()
 
     @steps(0, RING - 1)
@@ -497,19 +482,19 @@
 
     for offset in (1, 3, 2):
         x_ = mod(x + offset, 4)
-        landed(x_, pos_a, 0)
 
         @steps(1, RING)
         def _(i):
+            slot = mod(pos_a + i, RING)
             for g in range(2):
-                landed(x_, mod(pos_a + i, RING), g)
+                landed(red.at[core, x_, slot, g], t_recv.at[x_, slot, g])
 
         tc_copy(core, x_).start()
 
-    left(0, RING - 1, flows[0].s2)
-    left(1, 4 * (RING - 1), waits)
-    left(2, 3 * RING, waits)
-    left(3, 3, flows[0].s2)
+    left(0, 2 * (RING - 1), waits)
+    left(1, 3 * (RING - 1), waits)
+    left(2, 3 * (RING - 1), waits)
+    left(3, 2 * 3, waits)
 
     @steps(0, 4)
     def _(x_):

time: 67.6 us -> 68.5 us (1.013)
  Pallas kernels: 66.2 us -> 67.1 us
    pallas_call x1, Pallas kernels: 64.6 us -> 65.5 us  [per_device(): pl.pallas_call(kernel, out_shape=(jax.ShapeDtypeStruct((LON, LATENT), BF1...]
where the time goes in v6:
time: 68.5 us; the launch traced here: 68.4 us
  Pallas kernels  67.1 us (98%)
  between operations  1.29 us (2%)
    pallas_call x1, Pallas kernels, per_device(): pl.pallas_call(kernel, out_shape=(jax.ShapeDtypeStruct((LON, LATENT), BF1...  65.5 us
    pallas_call x1, Pallas kernels, per_device(): pl.pallas_call(unpack, out_shape=(jax.ShapeDtypeStruct((1, 1), F32), jax....  1.59 us

profile of v6, /device:TPU:1, one launch (start us, length us, event | category | flops | bytes accessed | tf_op | source)
XLA Modules:
  0.0 68.4 jit_solution(17463846981741017962)
XLA Ops:
  1.3 65.5 %decoder.1 = (bf16[720,512]{1,0:T(8,128)(2,1)S(1)}, bf16[2,4,8,2,16,256]{5,4,3,2,1,0:T(8,128)(2,1)S(1)}) custom-call(f32[8,128]{1,0:T(8,128)S(1)} %broadcast_in_dim.8.area_ref, bf16[720,512]{1,0:T(8,128)(2,1)} %bitcast.10, bf16[9,100,512]{2,1,0:T(8,128)(2,1)} %w_hbm.1, f32[45,1,100]{2,1,0:T(1,128)} %bitcast.12), custom_call_target="tpu_custom_call" | custom-call | flops 2600000000 | bytes 6000000 | tf_op jit(solution)/shard_map/decoder/pallas_call | solution.py:588
  66.8 1.6 %unpack.1 = (f32[1,1]{1,0:T(1,128)}, bf16[720,512]{1,0:T(8,128)(2,1)}, f32[9,100,512]{2,1,0:T(8,128)}) custom-call(bf16[720,512]{1,0:T(8,128)(2,1)S(1)} %get-tuple-element.8.d_ref, bf16[2,4,8,2,16,256]{5,4,3,2,1,0:T(8,128)(2,1)S(1)} %get-tuple-element.9.red), custom_call_target="tpu_custom_call" | custom-call | flops 1000000 | bytes 4500000 | tf_op jit(solution)/shard_map/unpack/pallas_call | solution.py:600
  (1 shorter events, 0.0 us)

commit v7 on v5

--- a/solution.py
+++ b/solution.py
@@ -479,11 +479,10 @@
             landed(x_, pos_a, 1)
             along_ring(1, x_)
 
+    from_x(1, 3)
     from_ring(1, 7)
-    from_x(1, 3)
-    from_ring(2, 6)
     from_x(2)
-    from_ring(3, 5, 4)
+    from_ring(2, 6, 3, 5, 4)
 
     @steps(1, RING)
     def _(i):

time: 67.6 us -> 67.2 us (level)
  no operation moved by 1% of the time
where the time goes in v7:
time: 67.2 us; the launch traced here: 67 us
  Pallas kernels  65.7 us (98%)
  between operations  1.29 us (2%)
    pallas_call x1, Pallas kernels, per_device(): pl.pallas_call(kernel, out_shape=(jax.ShapeDtypeStruct((LON, LATENT), BF1...  64.1 us
    pallas_call x1, Pallas kernels, per_device(): pl.pallas_call(unpack, out_shape=(jax.ShapeDtypeStruct((1, 1), F32), jax....  1.59 us

profile of v7, /device:TPU:1, one launch (start us, length us, event | category | flops | bytes accessed | tf_op | source)
XLA Modules:
  0.0 67.0 jit_solution(11597257582633657329)
XLA Ops:
  1.3 64.1 %decoder.1 = (bf16[720,512]{1,0:T(8,128)(2,1)S(1)}, bf16[2,4,8,2,16,256]{5,4,3,2,1,0:T(8,128)(2,1)S(1)}) custom-call(f32[8,128]{1,0:T(8,128)S(1)} %broadcast_in_dim.8.area_ref, bf16[720,512]{1,0:T(8,128)(2,1)} %bitcast.10, bf16[9,100,512]{2,1,0:T(8,128)(2,1)} %w_hbm.1, f32[45,1,100]{2,1,0:T(1,128)} %bitcast.12), custom_call_target="tpu_custom_call" | custom-call | flops 2600000000 | bytes 6000000 | tf_op jit(solution)/shard_map/decoder/pallas_call | solution.py:602
  65.4 1.6 %unpack.1 = (f32[1,1]{1,0:T(1,128)}, bf16[720,512]{1,0:T(8,128)(2,1)}, f32[9,100,512]{2,1,0:T(8,128)}) custom-call(bf16[720,512]{1,0:T(8,128)(2,1)S(1)} %get-tuple-element.8.d_ref, bf16[2,4,8,2,16,256]{5,4,3,2,1,0:T(8,128)(2,1)S(1)} %get-tuple-element.9.red), custom_call_target="tpu_custom_call" | custom-call | flops 1000000 | bytes 4500000 | tf_op jit(solution)/shard_map/unpack/pallas_call | solution.py:614
  (1 shorter events, 0.0 us)
